TPU v7x, 512 devices: a whole 4x8x8 slice. The times are simulated.
512 devices in a mesh: seq: 32 (over x, z), chan: 16 (over y, core).
Axes of the slice: x: 4, y: 8, z: 8, core: 2. Of those that a mesh axis runs over, the one named last changes fastest.
Arguments:
- gate_input: bfloat16 [4096, 8192], P('chan', 'seq'), may hold values from -6 to 6
- key_input: bfloat16 [4096, 8192], P('chan', 'seq'), may hold values from -6 to 6
- value_input: bfloat16 [4096, 8192], P('chan', 'seq'), may hold values from -6 to 6
- short_taps: float32 [9, 4096], P(None, 'chan'), may hold values from -3.5 to 3.5
- skip_gain: float32 [4096], P('chan'), may hold values from -3 to 3
- decay_rates: float32 [4096, 16], P('chan'), may hold values from 6.1035156e-05 to 0.05
- residues: float32 [4096, 16], P('chan'), may hold values from -2 to 2
- out_weight: bfloat16 [4096, 4096], P('chan'), may hold values from -0.09375 to 0.09375
Outputs:
- output: bfloat16 [4096, 8192], P('chan', 'seq')
All inputs are finite; a program needn't handle non-finite values.
Results may differ from a plain program's by a relative error of at most 0.0064.
Values may be sent and summed in bfloat16 or wider, within the bound.
A program may use at most 128 MiB of HBM per device.

v0:
```python
import math

import jax
import jax.numpy as jnp
from jax import lax
from jax.sharding import PartitionSpec as P

HIGH = lax.Precision.HIGHEST


def shifted(value, axis, by):
    length = lax.axis_size(axis)
    pairs = [(i, i + by) for i in range(length) if 0 <= i + by < length]
    return lax.ppermute(value, axis, pairs)


def tables(row_count, col_count):
    padded_len = row_count * col_count
    half_rows = row_count // 2
    row_freq = jnp.arange(row_count, dtype=jnp.int32)
    row_pos = jnp.arange(half_rows, dtype=jnp.int32)
    col_pos = jnp.arange(col_count, dtype=jnp.int32)
    row_angle = (
        2.0
        * math.pi
        / row_count
        * (row_freq[:, None] * row_pos[None, :] % row_count).astype(jnp.float32)
    )
    col_angle = (
        2.0
        * math.pi
        / col_count
        * (col_pos[:, None] * col_pos[None, :] % col_count).astype(jnp.float32)
    )
    twist_angle = (
        2.0
        * math.pi
        / padded_len
        * (row_freq[:, None] * col_pos[None, :] % padded_len).astype(jnp.float32)
    )
    return (
        jnp.cos(row_angle),
        jnp.sin(row_angle),
        jnp.cos(col_angle),
        jnp.sin(col_angle),
        jnp.cos(twist_angle),
        jnp.sin(twist_angle),
    )


def forward_dft(signal, row_count, col_count, table_set):
    cos_rows, sin_rows, cos_cols, sin_cols, twist_cos, twist_sin = table_set
    shaped = signal.reshape(signal.shape[0], row_count // 2, col_count)
    first_re = jnp.einsum("ka,cab->ckb", cos_rows, shaped, precision=HIGH)
    first_im = -jnp.einsum("ka,cab->ckb", sin_rows, shaped, precision=HIGH)
    turned_re = first_re * twist_cos + first_im * twist_sin
    turned_im = first_im * twist_cos - first_re * twist_sin
    spec_re = jnp.einsum("ckb,bd->ckd", turned_re, cos_cols, precision=HIGH) + jnp.einsum(
        "ckb,bd->ckd", turned_im, sin_cols, precision=HIGH
    )
    spec_im = jnp.einsum("ckb,bd->ckd", turned_im, cos_cols, precision=HIGH) - jnp.einsum(
        "ckb,bd->ckd", turned_re, sin_cols, precision=HIGH
    )
    return (spec_re, spec_im)


def inverse_dft(spec_re, spec_im, row_count, col_count, table_set):
    cos_rows, sin_rows, cos_cols, sin_cols, twist_cos, twist_sin = table_set
    inner_re = jnp.einsum("ckd,bd->ckb", spec_re, cos_cols, precision=HIGH) - jnp.einsum(
        "ckd,bd->ckb", spec_im, sin_cols, precision=HIGH
    )
    inner_im = jnp.einsum("ckd,bd->ckb", spec_im, cos_cols, precision=HIGH) + jnp.einsum(
        "ckd,bd->ckb", spec_re, sin_cols, precision=HIGH
    )
    turned_re = inner_re * twist_cos - inner_im * twist_sin
    turned_im = inner_im * twist_cos + inner_re * twist_sin
    result = jnp.einsum("ka,ckb->cab", cos_rows, turned_re, precision=HIGH) - jnp.einsum(
        "ka,ckb->cab", sin_rows, turned_im, precision=HIGH
    )
    return result.reshape(spec_re.shape[0], -1) / float(row_count * col_count)


def body(
    gate_input, key_input, value_input, short_taps, skip_gain, decay_rates, residues, out_weight
):
    chan_local, tok_local = gate_input.shape
    parts = lax.axis_size("seq")
    chan_block = chan_local // parts
    tokens_all = tok_local * parts
    padded_len = 2 * tokens_all
    col_count = 1
    while padded_len % (col_count * 4) == 0 and col_count * 2 * (col_count * 2) <= padded_len:
        col_count = col_count * 2
    row_count = padded_len // col_count
    stacked = jnp.stack([gate_input, key_input, value_input])
    prior = shifted(stacked[:, :, tok_local - 2 :], "seq", 1)
    extended = jnp.concatenate([prior, stacked], axis=2).astype(jnp.float32)
    taps = short_taps.reshape(3, 3, chan_local)
    shorts = []
    for proj_index in range(3):
        result = taps[proj_index, 0][:, None] * extended[proj_index, :, 2 : 2 + tok_local]
        for lag_steps in (1, 2):
            result = (
                result
                + taps[proj_index, lag_steps][:, None]
                * extended[proj_index, :, 2 - lag_steps : 2 - lag_steps + tok_local]
            )
        shorts.append(result)
    gate_short, key_short, value_short = shorts
    gated_input = (key_short * value_short).astype(jnp.bfloat16)
    relayed = lax.all_to_all(gated_input, "seq", split_axis=0, concat_axis=1, tiled=True)
    first_chan = lax.axis_index("seq") * chan_block
    rates = lax.dynamic_slice_in_dim(decay_rates, first_chan, chan_block, 0)
    weights_modes = lax.dynamic_slice_in_dim(residues, first_chan, chan_block, 0)
    gains = lax.dynamic_slice_in_dim(skip_gain, first_chan, chan_block, 0)
    positions = jnp.arange(tokens_all).astype(jnp.float32)
    filters = jnp.sum(
        weights_modes[:, :, None]
        * jnp.sqrt(rates)[:, :, None]
        * jnp.exp(-rates[:, :, None] * positions[None, None, :]),
        axis=1,
    )
    table_set = tables(row_count, col_count)
    wide_input = relayed.astype(jnp.float32)
    input_re, input_im = forward_dft(wide_input, row_count, col_count, table_set)
    filter_re, filter_im = forward_dft(filters, row_count, col_count, table_set)
    product_re = input_re * filter_re - input_im * filter_im
    product_im = input_re * filter_im + input_im * filter_re
    long_conv = inverse_dft(product_re, product_im, row_count, col_count, table_set)
    mixed = (long_conv + gains[:, None] * wide_input).astype(jnp.bfloat16)
    mixed_back = lax.all_to_all(mixed, "seq", split_axis=1, concat_axis=0, tiled=True)
    gated = (gate_short * mixed_back.astype(jnp.float32)).astype(jnp.bfloat16)
    projected = jnp.dot(
        out_weight,
        lax.all_gather(gated, "chan", axis=0, tiled=True),
        preferred_element_type=jnp.float32,
    )
    return projected.astype(jnp.bfloat16)


def solution(mesh):
    in_specs = (
        P("chan", "seq"),
        P("chan", "seq"),
        P("chan", "seq"),
        P(None, "chan"),
        P("chan"),
        P("chan", None),
        P("chan", None),
        P("chan", None),
    )
    out_specs = P("chan", "seq")
    return jax.shard_map(body, mesh=mesh, in_specs=in_specs, out_specs=out_specs, check_vma=False)
```

profile of v0, /device:TPU:1, one launch (start us, length us, event | category | flops | bytes accessed | tf_op | source)
XLA Modules:
  0.0 140.0 jit_solution(9321072165844178825)
XLA Ops:
  6.5 0.0 copy-start
  6.5 1.8 %pad_maximum_fusion = bf16[3,256,2]{2,1,0:T(8,128)(2,1)} fusion(bf16[1,256,256]{2,1,0:T(8,128)(2,1)} %bitcast.148, bf16[1,256,256]{2,1,0:T(8,128)(2,1)} %bitcast.150, bf16[1,256,256]{2,1,0:T(8,128)(2,1)} %bitcast.152), kind=kLoop, calls=%fused_computation.68 | loop fusion | flops 9216 | bytes 396288 | tf_op jit(solution)/shard_map/stack | solution.py:95
  8.4 5.5 %collective-permute-start = (bf16[3,256,2]{2,1,0:T(8,128)(2,1)}, bf16[3,256,2]{2,1,0:T(8,128)(2,1)}, u32[]{:S(2)}, u32[]{:S(2)}) collective-permute-start(bf16[3,256,2]{2,1,0:T(8,128)(2,1)} %pad_maximum_fusion), channel_id=1, source_target_pairs={{0,16},{16,32},{32,48},{48,64},{64,80},{80,96},{96,112},{112,128},... | collective-permute-start | bytes 9224 | tf_op jit(solution)/shard_map/ppermute | solution.py:14
  13.9 0.3 fusion.91
  14.1 0.3 fusion.90
  14.4 0.8 constant_dynamic-slice_fusion
  15.2 0.1 copy.155
  15.3 0.1 copy.154
  15.3 1.2 multiply_reduce_fusion
  16.6 1.1 fusion
  17.6 1.1 convolution_bitcast_fusion
  18.7 0.1 copy.118
  18.8 0.1 copy.119
  18.9 2.0 %fusion.41 = f32[8,128,128]{2,1,0:T(8,128)} fusion(f32[8,128,128]{1,2,0:T(8,128)S(1)} %convolution_bitcast_fusion, f32[8,128,128]{1,2,0:T(8,128)S(1)} %fusion, f32[128,128]{0,1:T(8,128)S(1)} %copy.119, f32[128,128]{0,1:T(8,128)S(1)} %copy.118), kind=kOutput, calls=%fused_computation.73 | convolution fusion | flops 201949184 | bytes 1703936 | tf_op jit(solution)/shard_map/ckb,bd->ckd/dot_general | solution.py:61
  20.9 2.0 %fusion.40 = f32[8,128,128]{2,1,0:T(8,128)} fusion(f32[8,128,128]{1,2,0:T(8,128)S(1)} %fusion, f32[8,128,128]{1,2,0:T(8,128)S(1)} %convolution_bitcast_fusion, f32[128,128]{0,1:T(8,128)S(1)} %copy.119, f32[128,128]{0,1:T(8,128)S(1)} %copy.118), kind=kOutput, calls=%fused_computation.72 | convolution fusion | flops 201949184 | bytes 1703936 | tf_op jit(solution)/shard_map/ckb,bd->ckd/dot_general | solution.py:58
  22.9 0.7 reshape.117
  23.6 3.0 %convolution_subtract_fusion.1 = f32[8,128,128]{2,1,0:T(8,128)} fusion(f32[8,128,128]{2,1,0:T(8,128)} %fusion.41, f32[8,128,128]{1,2,0:T(8,128)S(1)} %fusion, f32[8,128,128]{1,2,0:T(8,128)S(1)} %convolution_bitcast_fusion, f32[128,128]{0,1:T(8,128)S(1)} %copy.119, f32[128,128]{0,1:T(8,128)S(1)} %copy.118), kind=kOutput, calls=%fused_computation.9 | convolution fusion | flops 202080256 | bytes 2228224 | tf_op jit(solution)/shard_map/ckb,bd->ckd/dot_general | solution.py:61
  26.6 1.2 slice_reduce_fusion.5
  27.9 0.0 copy-done.11
  27.9 0.7 dynamic_slice.11
  28.5 0.8 mul.544
  29.3 1.4 mul.559
  30.6 1.4 mul.556
  32.0 1.4 mul.553
  33.4 1.3 mul.550
  34.7 1.4 mul.547
  36.1 0.0 collective-permute-done
  36.1 0.0 copy-done.5
  36.1 0.0 copy-done.6
  36.1 1.2 maximum_convert_fusion
  37.3 0.0 copy-start.1
  37.3 1.0 copy-done.1
  38.3 2.0 %fusion.15 = bf16[32,8,256]{2,1,0:T(8,128)(2,1)} fusion(f32[3,256,258]{2,1,0:T(8,128)S(1)} %maximum_convert_fusion, f32[32,8]{1,0:T(8,128)} %mul.559, f32[32,8]{1,0:T(8,128)} %mul.556, f32[32,8]{1,0:T(8,128)} %mul.553, f32[32,8]{1,0:T(8,128)} %mul.550, f32[32,8]{1,0:T(8,128)} %mul.547, f32[32,8]{1,0:T(8,128)S(1)} %mul.544), kind=kLoop, calls=%fused_computation.36 | loop fusion | flops 786432 | bytes 1710080 | tf_op jit(solution)/shard_map/convert_element_type | solution.py:110
  40.3 11.3 %all-to-all-start = ((bf16[32,8,256]{2,1,0:T(8,128)(2,1)}), bf16[32,8,256]{2,1,0:T(8,128)(2,1)S(1)}, u32[]{:S(2)}, u32[]{:S(2)}) async-start(bf16[32,8,256]{2,1,0:T(8,128)(2,1)} %fusion.15), calls=%async_computation | async-start | bytes 262144 | tf_op jit(solution)/shard_map/all_to_all | solution.py:111
  51.7 0.2 all-gather.2.cloned.1.call-start
  51.9 3.1 %convolution_add_fusion.1 = f32[8,128,128]{2,1,0:T(8,128)} fusion(f32[8,128,128]{2,1,0:T(8,128)} %fusion.40, f32[8,128,128]{1,2,0:T(8,128)S(1)} %convolution_bitcast_fusion, f32[8,128,128]{1,2,0:T(8,128)S(1)} %fusion, f32[128,128]{0,1:T(8,128)S(1)} %copy.119, f32[128,128]{0,1:T(8,128)S(1)} %copy.118), kind=kOutput, calls=%fused_computation.11 | convolution fusion | flops 202080256 | bytes 2228224 | tf_op jit(solution)/shard_map/ckb,bd->ckd/dot_general | solution.py:58
  55.0 5.9 %all-to-all-done = bf16[32,8,256]{2,1,0:T(8,128)(2,1)S(1)} async-done(((bf16[32,8,256]{2,1,0:T(8,128)(2,1)}), bf16[32,8,256]{2,1,0:T(8,128)(2,1)S(1)}, u32[]{:S(2)}, u32[]{:S(2)}) %all-to-all-start) | async-done | bytes 131104 | tf_op jit(solution)/shard_map/all_to_all | solution.py:111
  60.9 0.5 fusion.1
  61.4 0.5 convolution_bitcast_fusion.1
  62.0 1.2 fusion.39
  63.2 0.0 copy-start.3
  63.2 0.0 copy-start.4
  63.2 1.2 fusion.38
  64.4 1.2 convolution_add_fusion.2
  65.6 0.0 copy-done.3
  65.6 0.0 copy-done.4
  65.6 1.2 multiply_subtract_fusion
  66.8 0.9 fusion.54
  67.7 0.9 fusion.52
  68.6 0.9 convolution_subtract_fusion
  69.5 0.9 convolution_add_fusion
  70.4 0.0 copy-start.10
  70.5 0.9 fusion.8
  71.3 1.6 %fusion.3 = f32[8,64,128]{2,1,0:T(8,128)} fusion(f32[8,128,64]{1,2,0:T(8,128)S(1)} %fusion.8, f32[8,128,128]{1,2,0:T(8,128)S(1)} %convolution_subtract_fusion, f32[8,128,128]{1,2,0:T(8,128)S(1)} %convolution_add_fusion, f32[128,128]{0,1:T(8,128)S(1)} %copy.119, f32[128,128]{0,1:T(8,128)S(1)} %copy.118), kind=kOutput, calls=%fused_computation.15 | convolution fusion | flops 101302272 | bytes 1703936 | tf_op jit(solution)/shard_map/ka,ckb->cab/dot_general | solution.py:77
  72.9 1.7 %div.13 = f32[8,32,256]{2,1,0:T(8,128)} reshape(f32[8,64,128]{2,1,0:T(8,128)} %fusion.3) | data formatting | bytes 524288 | tf_op jit(solution)/shard_map/div | solution.py:80
  74.7 1.1 fusion.31
  75.8 12.7 %all_to_all.23 = bf16[8,32,256]{2,0,1:T(8,128)(2,1)S(1)} all-to-all(bf16[8,32,256]{2,0,1:T(8,128)(2,1)S(1)} %fusion.31), channel_id=1, replica_groups=mesh['seq'=32,'chan'=16] {'seq'}, dimensions={1} | all-to-all | bytes 262144 | tf_op jit(solution)/shard_map/all_to_all | solution.py:131
  88.5 0.0 copy-done.2
  88.5 0.0 copy-done.8
  88.5 1.0 fusion.27
  89.5 0.0 all-gather.2.cloned.1.call-update
  89.5 40.5 %all-gather.2.cloned.1.call-done = bf16[4096,256]{1,0:T(8,128)(2,1)} async-done(((bf16[256,256]{1,0:T(8,128)(2,1)}), bf16[4096,256]{1,0:T(8,128)(2,1)}) %all-gather.2.cloned.1.call-update) | async-done | bytes 2097168 | tf_op jit(solution)/shard_map/all_gather | solution.py:135
  130.1 2.3 %fusion.4 = bf16[256,256]{0,1:T(8,128)(2,1)S(1)} fusion(bf16[4096,256]{1,0:T(8,128)(2,1)} %all-gather.2.cloned.1.call-done, bf16[256,4096]{1,0:T(8,128)(2,1)S(1)} %copy-done), kind=kOutput, calls=%fused_computation.17 | convolution fusion | flops 536936448 | bytes 4325376 | tf_op jit(solution)/shard_map/dot_general | solution.py:133
  132.4 0.8 copy.139
  (15 shorter events, 0.1 us)
Async XLA Ops:
  6.5 123.5 %copy-start = (bf16[256,4096]{1,0:T(8,128)(2,1)S(1)}, bf16[256,4096]{1,0:T(8,128)(2,1)}, u32[]{:S(2)}) copy-start(bf16[256,4096]{1,0:T(8,128)(2,1)} %param.15) | copy-start | bytes 6291460
  8.4 27.7 %collective-permute-start = (bf16[3,256,2]{2,1,0:T(8,128)(2,1)}, bf16[3,256,2]{2,1,0:T(8,128)(2,1)}, u32[]{:S(2)}, u32[]{:S(2)}) collective-permute-start(bf16[3,256,2]{2,1,0:T(8,128)(2,1)} %pad_maximum_fusion), channel_id=1, source_target_pairs={{0,16},{16,32},{32,48},{48,64},{64,80},{80,96},{96,112},{112,128},... | collective-permute-start | bytes 9224 | tf_op jit(solution)/shard_map/ppermute | solution.py:14
  20.9 7.0 %copy-start.11 = (f32[256]{0:T(256)S(1)}, f32[256]{0:T(256)}, u32[]{:S(2)}) copy-start(f32[256]{0:T(256)} %param.12) | copy-start | bytes 3076
  20.9 15.2 %copy-start.5 = (bf16[256,256]{1,0:T(8,128)(2,1)S(1)}, bf16[256,256]{1,0:T(8,128)(2,1)}, u32[]{:S(2)}) copy-start(bf16[256,256]{1,0:T(8,128)(2,1)} %param.10) | copy-start | bytes 393220
  20.9 15.2 %copy-start.6 = (bf16[256,256]{1,0:T(8,128)(2,1)S(1)}, bf16[256,256]{1,0:T(8,128)(2,1)}, u32[]{:S(2)}) copy-start(bf16[256,256]{1,0:T(8,128)(2,1)} %param.9) | copy-start | bytes 393220
  37.3 1.0 copy-start.1
  40.3 20.5 %all-to-all-start = ((bf16[32,8,256]{2,1,0:T(8,128)(2,1)}), bf16[32,8,256]{2,1,0:T(8,128)(2,1)S(1)}, u32[]{:S(2)}, u32[]{:S(2)}) async-start(bf16[32,8,256]{2,1,0:T(8,128)(2,1)} %fusion.15), calls=%async_computation | async-start | bytes 262144 | tf_op jit(solution)/shard_map/all_to_all | solution.py:111
  51.7 78.4 %all-gather.2.cloned.1.call-start = ((), (), s32[]{:S(2)}) async-start(), calls=%async_computation.2 | async-start | bytes 2228224 | tf_op jit(solution)/shard_map/all_gather | solution.py:135
  63.2 2.4 %copy-start.3 = (f32[8,128,128]{2,1,0:T(8,128)S(1)}, f32[8,128,128]{2,1,0:T(8,128)}, u32[]{:S(2)}) copy-start(f32[8,128,128]{2,1,0:T(8,128)} %convolution_subtract_fusion.1) | copy-start | bytes 1572868
  63.2 2.4 %copy-start.4 = (f32[8,128,128]{2,1,0:T(8,128)S(1)}, f32[8,128,128]{2,1,0:T(8,128)}, u32[]{:S(2)}) copy-start(f32[8,128,128]{2,1,0:T(8,128)} %convolution_add_fusion.1) | copy-start | bytes 1572868
  70.4 4.3 %copy-start.10 = (f32[8]{0:T(128)S(1)}, f32[8]{0:T(128)}, u32[]{:S(2)}) copy-start(f32[8]{0:T(128)} %dynamic_slice.11) | copy-start | bytes 100
  70.4 18.1 %copy-start.2 = (f32[3,256,258]{2,1,0:T(8,128)S(1)}, f32[3,256,258]{2,1,0:T(8,128)}, u32[]{:S(2)}) copy-start(f32[3,256,258]{2,1,0:T(8,128)} %copy-done.1) | copy-start | bytes 2377732
  70.4 18.1 %copy-start.7 = (f32[1,1,256]{2,1,0:T(1,128)S(1)}, f32[1,1,256]{2,1,0:T(1,128)}, u32[]{:S(2)}) copy-start(f32[1,1,256]{2,1,0:T(1,128)} %get-tuple-element.13) | copy-start | bytes 3076
  70.4 18.1 %copy-start.8 = (f32[1,1,256]{2,1,0:T(1,128)S(1)}, f32[1,1,256]{2,1,0:T(1,128)}, u32[]{:S(2)}) copy-start(f32[1,1,256]{2,1,0:T(1,128)} %get-tuple-element.14) | copy-start | bytes 3076
  70.4 18.1 %copy-start.9 = (f32[1,1,256]{2,1,0:T(1,128)S(1)}, f32[1,1,256]{2,1,0:T(1,128)}, u32[]{:S(2)}) copy-start(f32[1,1,256]{2,1,0:T(1,128)} %get-tuple-element.15) | copy-start | bytes 3076
Sparse Core Ops, SparseCore 0:
  89.7 40.3 all-gather.1
where the time goes:
time: 141 us; the launch traced here: 140 us
  waiting for transfers between devices  46.4 us (33%)
  matrix products  26.4 us (19%)
  starting transfers between devices  17 us (12%)
  local copies, waits for them, and re-layouts  14.9 us (11%)
  between operations  13.7 us (10%)
  blocking collectives  12.7 us (9%)
  other arithmetic  8.9 us (6%)
    all_gather x1, waiting for transfers between devices, body(): lax.all_gather(gated, 'chan', axis=0, tiled=True)  40.5 us
    all_to_all x1, blocking collectives, body(): lax.all_to_all(mixed, 'seq', split_axis=1, concat_axis=0, tiled=True)  12.7 us
    all_to_all x1, starting transfers between devices, body(): lax.all_to_all(gated_input, 'seq', split_axis=0, concat_axis=1, tiled=True)  11.3 us
    all_to_all x1, waiting for transfers between devices, body(): lax.all_to_all(gated_input, 'seq', split_axis=0, concat_axis=1, tiled=True)  5.88 us
    ppermute x1, starting transfers between devices, shifted(): return lax.ppermute(value, axis, pairs)  5.5 us
    mul x4, local copies, waits for them, and re-layouts, body(): taps[proj_index, lag_steps][:, None]  5.43 us
    dot_general x2, matrix products, forward_dft(): jnp.einsum('ckb,bd->ckd', turned_im, sin_cols, precision=HIGH)  4.26 us
    dot_general x2, matrix products, forward_dft(): jnp.einsum('ckb,bd->ckd', turned_re, sin_cols, precision=HIGH)  4.22 us
  transfers between devices with their start and end apart: 3, of which 2 were waited for; matrix products, arithmetic and copies ran while one was open for 18% of the time, Pallas kernels for 0%

commit v1 on v0

v1 whole, which is shorter than its diff:
```python
import functools
import math

import jax
import jax.numpy as jnp
from jax import lax
from jax.experimental import pallas as pl
from jax.experimental.pallas import tpu as pltpu
from jax.sharding import PartitionSpec as P

MESH = pl.DeviceIdType.MESH
F32 = jnp.float32
BF16 = jnp.bfloat16
NZ = 8
MODES = 16
CHUNKS = 8
LANES = 128
MSG = 24


def rounded(value):
    return value.astype(BF16).astype(F32)


def kernel(
    nseq,
    nchan,
    gate_hbm,
    key_hbm,
    value_hbm,
    taps_ref,
    gain_ref,
    rates_ref,
    res_ref,
    weight_hbm,
    out_ref,
    gate_v,
    key_v,
    value_v,
    weight_v,
    perm,
    ext,
    u_ref,
    gs_ref,
    y_ref,
    gt_ref,
    a_rep,
    w_rep,
    cin,
    zbuf,
    xbuf,
    tmsg,
    gmsg,
    gbuf,
    carry,
    gathered,
    acc,
    in_sem,
    z_s,
    z_r,
    x_s,
    x_r,
    g_s,
    g_r,
    ring_s,
    ring_r,
    sib_s,
    sib_r,
):
    nx = nseq // NZ
    ny = nchan // 2
    half = ny // 2
    toks = gate_v.shape[1]
    chans = gate_v.shape[0]
    blocks = toks // CHUNKS
    halves = chans // LANES
    seq = lax.axis_index("seq")
    chan = lax.axis_index("chan")
    x, z = seq // NZ, seq % NZ
    y, core = chan // 2, chan % 2
    sibling = chan + 1 - 2 * core

    loads = []
    for n, (src, dst) in enumerate(
        ((key_hbm, key_v), (value_hbm, value_v), (gate_hbm, gate_v), (weight_hbm, weight_v))
    ):
        copy = pltpu.make_async_copy(src, dst, in_sem.at[n])
        copy.start()
        loads.append(copy)

    z_peers = [x * NZ + (z + d) % NZ for d in range(1, NZ)]
    x_peers = [((x + d) % nx) * NZ + z for d in range(1, nx)]
    after, before = (seq + 1) % nseq, (seq + nseq - 1) % nseq
    above = ((y + 1) % ny) * 2 + core
    below = ((y + ny - 1) % ny) * 2 + core

    barrier = pltpu.get_barrier_semaphore()
    peers = [(s, chan) for s in z_peers + x_peers + [after, before]]
    peers += [(seq, c) for c in (above, below, sibling)]
    for peer in peers:
        pl.semaphore_signal(barrier, inc=1, device_id=peer, device_id_type=MESH)

    row = lax.broadcasted_iota(jnp.int32, (toks, toks), 0)
    col = lax.broadcasted_iota(jnp.int32, (toks, toks), 1)
    perm[...] = jnp.where(col == (row % CHUNKS) * blocks + row // CHUNKS, 1.0, 0.0).astype(BF16)

    def nt(lhs, rhs, precision=None):
        return lax.dot_general(
            lhs, rhs, (((1,), (1,)), ((), ())), precision=precision, preferred_element_type=F32
        )

    pick_rep = jnp.where(
        lax.broadcasted_iota(jnp.int32, (MODES * CHUNKS, MODES), 0) // CHUNKS
        == lax.broadcasted_iota(jnp.int32, (MODES * CHUNKS, MODES), 1),
        1.0,
        0.0,
    )
    pick = jnp.where(
        lax.broadcasted_iota(jnp.int32, (MODES, MODES), 0)
        == lax.broadcasted_iota(jnp.int32, (MODES, MODES), 1),
        1.0,
        0.0,
    )
    rates = rates_ref[...]
    weights = res_ref[...] * jnp.sqrt(rates)
    high = lax.Precision.HIGHEST
    r_rep = nt(pick_rep, rates, high)
    a_rep[...] = jnp.exp(-r_rep).reshape(MODES, CHUNKS, chans)
    w_rep[...] = nt(pick_rep, weights, high).reshape(MODES, CHUNKS, chans)
    r_c = nt(pick, rates, high)
    w_c = nt(pick, weights, high)

    first = lax.broadcasted_iota(jnp.int32, (CHUNKS, chans), 0) == 0
    tail = CHUNKS * (blocks - 2)

    def short(which, source):
        loads[which].wait()
        laid = nt(perm[...], source[...])
        m = (1, 2, 0)[which]
        tap = [taps_ref[3 * m + j : 3 * m + j + 1, :] for j in range(3)]
        ext[2 * CHUNKS :, :] = laid
        for n in range(2):
            block = laid[tail + n * CHUNKS : tail + (n + 1) * CHUNKS]
            ext[n * CHUNKS : (n + 1) * CHUNKS, :] = jnp.where(first, 0.0, pltpu.roll(block, 1, 0))
        result = tap[0] * laid
        result = result + tap[1] * ext[CHUNKS : CHUNKS + toks, :]
        result = result + tap[2] * ext[0:toks, :]
        last = laid[toks - 1 : toks]
        prev = laid[toks - 1 - CHUNKS : toks - CHUNKS]
        return result, tap[1] * last + tap[2] * prev, tap[2] * last

    own = zbuf.at[z]
    key_short, q0, q1 = short(0, key_v)
    own[16:17, :] = key_short[0:1]
    own[17:18, :] = key_short[CHUNKS : CHUNKS + 1]
    own[20:21, :] = q0
    own[21:22, :] = q1
    value_short, q0, q1 = short(1, value_v)
    own[18:19, :] = value_short[0:1]
    own[19:20, :] = value_short[CHUNKS : CHUNKS + 1]
    own[22:23, :] = q0
    own[23:24, :] = q1
    u_ref[...] = rounded(key_short * value_short)
    for n in range(2):
        u_ref[n * CHUNKS : n * CHUNKS + 1, :] = jnp.zeros((1, chans), F32)

    k3 = lax.broadcasted_iota(jnp.int32, (MODES, CHUNKS, LANES), 1)
    for h in range(halves):
        lanes = slice(h * LANES, (h + 1) * LANES)
        a = a_rep[:, :, lanes]

        def scan(i, state):
            u = u_ref[pl.ds(pl.multiple_of(i * CHUNKS, CHUNKS), CHUNKS), lanes]
            return state * a + u[None]

        state = lax.fori_loop(0, blocks, scan, jnp.zeros((MODES, CHUNKS, LANES), F32), unroll=8)
        step = a
        for _ in range(int(math.log2(blocks))):
            step = step * step
        shift = 1
        while shift < CHUNKS:
            moved = jnp.where(k3 >= shift, pltpu.roll(state, shift, 1), 0.0)
            state = state + step * moved
            step = step * step
            shift *= 2
        cin[:, :, lanes] = jnp.where(k3 >= 1, pltpu.roll(state, 1, 1), 0.0)
        for s in range(MODES):
            own[s : s + 1, lanes] = state[s, CHUNKS - 1 : CHUNKS, :]

    pl.semaphore_wait(barrier, len(peers))

    def send(src, dst, ssem, rsem, peer):
        copy = pltpu.make_async_remote_copy(
            src_ref=src,
            dst_ref=dst,
            send_sem=ssem,
            recv_sem=rsem,
            device_id=peer,
            device_id_type=MESH,
        )
        copy.start()
        return copy

    sent = []
    for n, peer in enumerate(z_peers):
        sent.append(send(own, own, z_s.at[n], z_r.at[n], (peer, chan)))

    gate_short, q0, q1 = short(2, gate_v)
    gs_ref[...] = gate_short
    gmsg[...] = jnp.zeros_like(gmsg)
    gmsg[0:1, :] = q0
    gmsg[1:2, :] = q1
    sent.append(send(gmsg, gbuf, g_s.at[0], g_r.at[0], (after, chan)))

    for h in range(halves):
        lanes = slice(h * LANES, (h + 1) * LANES)
        a = a_rep[:, :, lanes]
        w = w_rep[:, :, lanes]

        def local(i, state):
            rows = pl.ds(pl.multiple_of(i * CHUNKS, CHUNKS), CHUNKS)
            state = state * a + u_ref[rows, lanes][None]
            y_ref[rows, lanes] = jnp.sum(state * w, axis=0)
            return state

        lax.fori_loop(0, blocks, local, jnp.zeros((MODES, CHUNKS, LANES), F32), unroll=4)

    def decay(count):
        return jnp.exp(-r_c * count)

    def edge_tokens(q, msg):
        u0 = rounded((msg[16:17] + q[0:1]) * (msg[18:19] + q[2:3]))
        u1 = rounded((msg[17:18] + q[1:2]) * (msg[19:20] + q[3:4]))
        return u0, u1

    def arrival(buf, index, rsem):
        return pltpu.make_async_remote_copy(
            src_ref=buf.at[index],
            dst_ref=buf.at[index],
            send_sem=z_s.at[0],
            recv_sem=rsem,
            device_id=(seq, chan),
            device_id_type=MESH,
        )

    span = float(toks)
    d0, d1, d2 = decay(span), decay(span - 1.0), decay(span - 2.0)
    e0, e1, e2 = decay(NZ * span), decay(NZ * span - 1.0), decay(NZ * span - 2.0)
    for n in range(NZ - 1):
        arrival(zbuf, (z + NZ - 1 - n) % NZ, z_r.at[n]).wait_recv()
    msg = zbuf[0]
    cur, q = msg[:MODES], msg[20:24]
    zero = jnp.zeros((MODES, chans), F32)
    mine, mine_q = zero, jnp.zeros((4, chans), F32)
    for n in range(1, NZ):
        here = z == n
        mine = jnp.where(here, cur, mine)
        mine_q = jnp.where(here, q, mine_q)
        msg = zbuf[n]
        u0, u1 = edge_tokens(q, msg)
        cur = d0 * cur + msg[:MODES] + d1 * u0 + d2 * u1
        q = msg[20:24]
    tmsg[0:MODES, :] = cur
    tmsg[16:20, :] = zbuf[0, 16:20, :]
    tmsg[20:24, :] = q
    for n, peer in enumerate(x_peers):
        sent.append(send(tmsg, xbuf.at[x], x_s.at[n], x_r.at[n], (peer, chan)))

    for n in range(nx - 1):
        arrival(xbuf, (x + nx - 1 - n) % nx, x_r.at[n]).wait_recv()
    cur, q = zero, jnp.zeros((4, chans), F32)
    for n in range(nx - 1):
        use = n < x
        msg = xbuf[n]
        u0, u1 = edge_tokens(q, msg)
        new = e0 * cur + msg[:MODES] + e1 * u0 + e2 * u1
        cur = jnp.where(use, new, cur)
        q = jnp.where(use, msg[20:24], q)
    u0, u1 = edge_tokens(q, zbuf[0])
    ahead = z.astype(F32) * span
    inside = mine + decay(ahead) * cur + decay(ahead - 1.0) * u0 + decay(ahead - 2.0) * u1
    at_first = z == 0
    state_in = jnp.where(at_first, cur, inside)
    q = jnp.where(at_first, q, mine_q)
    u0, u1 = edge_tokens(q, own)
    u_ref[0:1, :] = u0
    u_ref[CHUNKS : CHUNKS + 1, :] = u1
    back = jnp.exp(r_c)
    carry[...] = state_in + back * u0 + back * back * u1
    y_ref[0:1, :] = y_ref[0:1, :] - jnp.sum(w_c * back, axis=0, keepdims=True) * u1
    pltpu.make_async_remote_copy(
        src_ref=gmsg,
        dst_ref=gbuf,
        send_sem=g_s.at[0],
        recv_sem=g_r.at[0],
        device_id=(seq, chan),
        device_id_type=MESH,
    ).wait_recv()
    begins = seq == 0
    for n in range(2):
        at = slice(n * CHUNKS, n * CHUNKS + 1)
        gs_ref[at, :] = gs_ref[at, :] + jnp.where(begins, 0.0, gbuf[n : n + 1, :])

    def piece_of(c, h):
        return gathered.at[c, pl.ds(h * LANES, LANES)]

    def goes(way, hop, h):
        return hop < half or (hop == half and h % 2 == way)

    def forward(way, hop, h, c):
        block = piece_of(c, h)
        peer = (seq, (above, below)[way])
        sem = (way, hop - 1, h)
        sent.append(send(block, block, ring_s.at[sem], ring_r.at[sem], peer))

    def share(slot, h, c):
        block = piece_of(c, h)
        sem = (slot, h)
        sent.append(send(block, block, sib_s.at[sem], sib_r.at[sem], (seq, sibling)))

    def wait_block(c, h, rsem):
        block = piece_of(c, h)
        pltpu.make_async_remote_copy(
            src_ref=block,
            dst_ref=block,
            send_sem=z_s.at[0],
            recv_sem=rsem,
            device_id=(seq, chan),
            device_id_type=MESH,
        ).wait_recv()

    k8 = lax.broadcasted_iota(jnp.int32, (CHUNKS, LANES), 0).astype(F32) * float(blocks)
    for h in range(halves):
        lanes = slice(h * LANES, (h + 1) * LANES)
        a = a_rep[:, :, lanes]
        lead = jnp.stack(
            [
                jnp.broadcast_to(carry[s : s + 1, lanes], (CHUNKS, LANES))
                * jnp.exp(-jnp.broadcast_to(r_c[s : s + 1, lanes], (CHUNKS, LANES)) * k8)
                for s in range(MODES)
            ]
        )
        start = w_rep[:, :, lanes] * a * (lead + cin[:, :, lanes])
        gain = gain_ref[:, lanes]

        def finish(i, state):
            rows = pl.ds(pl.multiple_of(i * CHUNKS, CHUNKS), CHUNKS)
            conv = y_ref[rows, lanes] + jnp.sum(state, axis=0)
            mixed = rounded(conv + gain * u_ref[rows, lanes])
            gt_ref[rows, :] = gs_ref[rows, lanes] * mixed
            return state * a

        lax.fori_loop(0, blocks, finish, start, unroll=4)
        gathered[chan, h * LANES : (h + 1) * LANES, :] = lax.dot_general(
            gt_ref[...].astype(BF16),
            perm[...],
            (((0,), (0,)), ((), ())),
            preferred_element_type=F32,
        ).astype(BF16)
        for way in range(2):
            if goes(way, 1, h):
                forward(way, 1, h, chan)
        share(0, h, chan)

    loads[3].wait()

    def product(c):
        cols = pl.ds(pl.multiple_of(c * chans, chans), chans)
        return jnp.dot(weight_v[:, cols], gathered[c], preferred_element_type=F32)

    def other(c):
        return c + 1 - 2 * core

    acc[...] = product(chan)
    for h in range(halves):
        wait_block(sibling, h, sib_r.at[0, h])
    acc[...] += product(sibling)
    for hop in range(1, half + 1):
        origins = [((y + ny - hop) % ny) * 2 + core, ((y + hop) % ny) * 2 + core]
        for h in range(halves):
            for way in range(2):
                if goes(way, hop, h):
                    c = origins[way]
                    wait_block(c, h, ring_r.at[way, hop - 1, h])
                    if goes(way, hop + 1, h):
                        forward(way, hop + 1, h, c)
                    share(1 + way * half + hop - 1, h, c)
        arrived = origins if hop < half else origins[:1]
        total = product(arrived[0])
        for c in arrived[1:]:
            total += product(c)
        acc[...] += total
        for h in range(halves):
            for way in range(2):
                if goes(way, hop, h):
                    wait_block(other(origins[way]), h, sib_r.at[1 + way * half + hop - 1, h])
        total = product(other(arrived[0]))
        for c in arrived[1:]:
            total += product(other(c))
        if hop < half:
            acc[...] += total
        else:
            out_ref[...] = (acc[...] + total).astype(BF16)
    for copy in sent:
        copy.wait_send()


def body(nseq, nchan, gate, key, value, taps, gain, rates, residues, weight):
    chans, toks = gate.shape
    half = nchan // 4
    vmem = pl.BlockSpec(memory_space=pltpu.VMEM)
    anywhere = pl.BlockSpec(memory_space=pl.ANY)
    dma = pltpu.SemaphoreType.DMA
    nx = nseq // NZ
    return pl.pallas_call(
        functools.partial(kernel, nseq, nchan),
        out_shape=jax.ShapeDtypeStruct((weight.shape[0], toks), BF16),
        in_specs=[anywhere] * 3 + [vmem] * 4 + [anywhere],
        out_specs=vmem,
        scratch_shapes=[
            pltpu.VMEM((chans, toks), BF16),
            pltpu.VMEM((chans, toks), BF16),
            pltpu.VMEM((chans, toks), BF16),
            pltpu.VMEM(weight.shape, BF16),
            pltpu.VMEM((toks, toks), BF16),
            pltpu.VMEM((toks + 2 * CHUNKS, chans), F32),
            pltpu.VMEM((toks, chans), F32),
            pltpu.VMEM((toks, chans), F32),
            pltpu.VMEM((toks, chans), F32),
            pltpu.VMEM((toks, LANES), F32),
            pltpu.VMEM((MODES, CHUNKS, chans), F32),
            pltpu.VMEM((MODES, CHUNKS, chans), F32),
            pltpu.VMEM((MODES, CHUNKS, chans), F32),
            pltpu.VMEM((NZ, MSG, chans), F32),
            pltpu.VMEM((nx, MSG, chans), F32),
            pltpu.VMEM((MSG, chans), F32),
            pltpu.VMEM((8, chans), F32),
            pltpu.VMEM((8, chans), F32),
            pltpu.VMEM((MODES, chans), F32),
            pltpu.VMEM((nchan, chans, toks), BF16),
            pltpu.VMEM((weight.shape[0], toks), F32),
            dma((4,)),
            dma((NZ - 1,)),
            dma((NZ - 1,)),
            dma((max(nx - 1, 1),)),
            dma((max(nx - 1, 1),)),
            dma((1,)),
            dma((1,)),
            dma((2, half, 2)),
            dma((2, half, 2)),
            dma((1 + 2 * half, 2)),
            dma((1 + 2 * half, 2)),
        ],
        compiler_params=pltpu.CompilerParams(
            collective_id=0, has_side_effects=True, vmem_limit_bytes=40 * 1024 * 1024
        ),
        name="hyena",
    )(gate, key, value, taps, gain.reshape(1, -1), rates, residues, weight)


def solution(mesh):
    in_specs = (
        P("chan", "seq"),
        P("chan", "seq"),
        P("chan", "seq"),
        P(None, "chan"),
        P("chan"),
        P("chan", None),
        P("chan", None),
        P("chan", None),
    )
    return jax.shard_map(
        functools.partial(body, mesh.shape["seq"], mesh.shape["chan"]),
        mesh=mesh,
        in_specs=in_specs,
        out_specs=P("chan", "seq"),
        check_vma=False,
    )
```

time: 141 us -> 52.4 us (0.37)
  waiting for transfers between devices: 46.4 us -> 0 us
  Pallas kernels: 0 us -> 44 us
  matrix products: 26.4 us -> 0 us
  starting transfers between devices: 17 us -> 0 us
  between operations: 13.7 us -> 0.02 us
  blocking collectives: 12.7 us -> 0 us
  other arithmetic: 8.9 us -> 0 us
  local copies, waits for them, and re-layouts: 14.9 us -> 7.98 us
    pallas_call x0 -> x1, Pallas kernels: none -> 44 us  [body(): pl.pallas_call(functools.partial(kernel, nseq, nchan), out_shape=jax.Shap...]
    all_gather x1 -> x0, waiting for transfers between devices: 40.5 us -> none  [body(): lax.all_gather(gated, 'chan', axis=0, tiled=True)]
    dot_general x19 -> x0, matrix products: 26.4 us -> none  [the longest x2 4.26 us: forward_dft(): jnp.einsum('ckb,bd->ckd', turned_im, sin_cols, precision=HIGH)]
    all_to_all x1 -> x0, blocking collectives: 12.7 us -> none  [body(): lax.all_to_all(mixed, 'seq', split_axis=1, concat_axis=0, tiled=True)]
    all_to_all x1 -> x0, starting transfers between devices: 11.3 us -> none  [body(): lax.all_to_all(gated_input, 'seq', split_axis=0, concat_axis=1, tiled=True)]
    mul x6 -> x0, local copies, waits for them, and re-layouts: 7.55 us -> none  [the longest x4 5.43 us: body(): taps[proj_index, lag_steps][:, None]]
    unnamed x26 -> x15, local copies, waits for them, and re-layouts: 1.18 us -> 7.98 us
    all_to_all x1 -> x0, waiting for transfers between devices: 5.88 us -> none  [body(): lax.all_to_all(gated_input, 'seq', split_axis=0, concat_axis=1, tiled=True)]
  transfers between devices with their start and end apart: 3 -> 0, of which waited for: 2 -> 0; matrix products, arithmetic and copies ran while one was open for 18% -> 0% of each run, Pallas kernels for 0% -> 0%
where the time goes in v1:
time: 52.4 us; the launch traced here: 52.1 us
  Pallas kernels  44 us (84%)
  local copies, waits for them, and re-layouts  7.98 us (15%)
    pallas_call x1, Pallas kernels, body(): pl.pallas_call(functools.partial(kernel, nseq, nchan), out_shape=jax.Shap...  44 us
    unnamed x15, local copies, waits for them, and re-layouts  7.98 us

profile of v1, /device:TPU:1, one launch (start us, length us, event | category | flops | bytes accessed | tf_op | source)
XLA Modules:
  0.0 52.1 jit_solution(9507838076766077418)
XLA Ops:
  0.0 0.8 %copy.9.rates_ref = f32[256,16]{1,0:T(8,128)S(1)} copy(f32[256,16]{0,1:T(8,128)} %param.13) | data formatting | bytes 32768 | tf_op args[5]
  0.8 0.8 %copy.10.res_ref = f32[256,16]{1,0:T(8,128)S(1)} copy(f32[256,16]{0,1:T(8,128)} %param.14) | data formatting | bytes 32768 | tf_op args[6]
  1.6 0.0 copy-start
  1.6 1.6 %copy-done = bf16[256,4096]{1,0:T(8,128)(2,1)S(1)} copy-done((bf16[256,4096]{1,0:T(8,128)(2,1)S(1)}, bf16[256,4096]{1,0:T(8,128)(2,1)}, u32[]{:S(2)}) %copy-start) | copy-done | bytes 2097176
  3.2 0.0 copy-start.1
  3.2 0.9 %copy-done.1 = bf16[256,256]{1,0:T(8,128)(2,1)S(1)} copy-done((bf16[256,256]{1,0:T(8,128)(2,1)S(1)}, bf16[256,256]{1,0:T(8,128)(2,1)}, u32[]{:S(2)}) %copy-start.1) | copy-done | bytes 131096
  4.1 0.0 copy-start.2
  4.1 0.9 %copy-done.2 = bf16[256,256]{1,0:T(8,128)(2,1)S(1)} copy-done((bf16[256,256]{1,0:T(8,128)(2,1)S(1)}, bf16[256,256]{1,0:T(8,128)(2,1)}, u32[]{:S(2)}) %copy-start.2) | copy-done | bytes 131096
  5.0 0.0 copy-start.3
  5.0 0.9 %copy-done.3 = bf16[256,256]{1,0:T(8,128)(2,1)S(1)} copy-done((bf16[256,256]{1,0:T(8,128)(2,1)S(1)}, bf16[256,256]{1,0:T(8,128)(2,1)}, u32[]{:S(2)}) %copy-start.3) | copy-done | bytes 131096
  5.9 0.0 copy-start.4
  5.9 0.7 %copy-done.4 = f32[9,256]{1,0:T(8,128)S(1)} copy-done((f32[9,256]{1,0:T(8,128)S(1)}, f32[9,256]{1,0:T(8,128)}, u32[]{:S(2)}) %copy-start.4) | copy-done | bytes 9240
  6.7 0.0 copy-start.5
  6.7 0.7 %copy-done.5 = f32[256]{0:T(256)S(1)} copy-done((f32[256]{0:T(256)S(1)}, f32[256]{0:T(256)}, u32[]{:S(2)}) %copy-start.5) | copy-done | bytes 1048
  7.3 44.0 %hyena.1 = bf16[256,256]{1,0:T(8,128)(2,1)S(1)} custom-call(bf16[256,256]{1,0:T(8,128)(2,1)S(1)} %copy-done.1, bf16[256,256]{1,0:T(8,128)(2,1)S(1)} %copy-done.2, bf16[256,256]{1,0:T(8,128)(2,1)S(1)} %copy-done.3, f32[9,256]{1,0:T(8,128)S(1)} %copy-done.4, f32[1,256]{1,0:T(1,128)S(1)} %bitcast.1, f32[256,16]{1,0:T(8,128)S(1)} %copy.9.rates_ref, ...), custom_call_target="tpu_custom_call" | custom-call | tf_op jit(solution)/shard_map/hyena/pallas_call | solution.py:415
  51.4 0.7 %copy.12 = bf16[256,256]{1,0:T(8,128)(2,1)} copy(bf16[256,256]{1,0:T(8,128)(2,1)S(1)} %hyena.1) | data formatting | bytes 262144
Async XLA Ops:
  1.6 1.6 %copy-start = (bf16[256,4096]{1,0:T(8,128)(2,1)S(1)}, bf16[256,4096]{1,0:T(8,128)(2,1)}, u32[]{:S(2)}) copy-start(bf16[256,4096]{1,0:T(8,128)(2,1)} %weight_hbm.1) | copy-start | bytes 6291460
  3.2 0.9 %copy-start.1 = (bf16[256,256]{1,0:T(8,128)(2,1)S(1)}, bf16[256,256]{1,0:T(8,128)(2,1)}, u32[]{:S(2)}) copy-start(bf16[256,256]{1,0:T(8,128)(2,1)} %gate_hbm.1) | copy-start | bytes 393220
  4.1 0.9 %copy-start.2 = (bf16[256,256]{1,0:T(8,128)(2,1)S(1)}, bf16[256,256]{1,0:T(8,128)(2,1)}, u32[]{:S(2)}) copy-start(bf16[256,256]{1,0:T(8,128)(2,1)} %key_hbm.1) | copy-start | bytes 393220
  5.0 0.9 %copy-start.3 = (bf16[256,256]{1,0:T(8,128)(2,1)S(1)}, bf16[256,256]{1,0:T(8,128)(2,1)}, u32[]{:S(2)}) copy-start(bf16[256,256]{1,0:T(8,128)(2,1)} %value_hbm.1) | copy-start | bytes 393220
  5.9 0.7 %copy-start.4 = (f32[9,256]{1,0:T(8,128)S(1)}, f32[9,256]{1,0:T(8,128)}, u32[]{:S(2)}) copy-start(f32[9,256]{1,0:T(8,128)} %taps_ref.1) | copy-start | bytes 27652
  6.7 0.7 %copy-start.5 = (f32[256]{0:T(256)S(1)}, f32[256]{0:T(256)}, u32[]{:S(2)}) copy-start(f32[256]{0:T(256)} %param.12) | copy-start | bytes 3076

commit v2 on v1

--- a/solution.py
+++ b/solution.py
@@ -28,12 +28,16 @@
     gate_hbm,
     key_hbm,
     value_hbm,
-    taps_ref,
-    gain_ref,
-    rates_ref,
-    res_ref,
+    taps_hbm,
+    gain_hbm,
+    rates_hbm,
+    res_hbm,
     weight_hbm,
     out_ref,
+    taps_v,
+    gain_v,
+    rates_v,
+    res_v,
     gate_v,
     key_v,
     value_v,
@@ -82,7 +86,16 @@
 
     loads = []
     for n, (src, dst) in enumerate(
-        ((key_hbm, key_v), (value_hbm, value_v), (gate_hbm, gate_v), (weight_hbm, weight_v))
+        (
+            (rates_hbm, rates_v),
+            (res_hbm, res_v),
+            (taps_hbm, taps_v),
+            (key_hbm, key_v),
+            (value_hbm, value_v),
+            (gate_hbm, gate_v),
+            (gain_hbm, gain_v),
+            (weight_hbm, weight_v),
+        )
     ):
         copy = pltpu.make_async_copy(src, dst, in_sem.at[n])
         copy.start()
@@ -109,35 +122,25 @@
             lhs, rhs, (((1,), (1,)), ((), ())), precision=precision, preferred_element_type=F32
         )
 
-    pick_rep = jnp.where(
-        lax.broadcasted_iota(jnp.int32, (MODES * CHUNKS, MODES), 0) // CHUNKS
-        == lax.broadcasted_iota(jnp.int32, (MODES * CHUNKS, MODES), 1),
-        1.0,
-        0.0,
-    )
-    pick = jnp.where(
-        lax.broadcasted_iota(jnp.int32, (MODES, MODES), 0)
-        == lax.broadcasted_iota(jnp.int32, (MODES, MODES), 1),
-        1.0,
-        0.0,
-    )
-    rates = rates_ref[...]
-    weights = res_ref[...] * jnp.sqrt(rates)
-    high = lax.Precision.HIGHEST
-    r_rep = nt(pick_rep, rates, high)
-    a_rep[...] = jnp.exp(-r_rep).reshape(MODES, CHUNKS, chans)
-    w_rep[...] = nt(pick_rep, weights, high).reshape(MODES, CHUNKS, chans)
-    r_c = nt(pick, rates, high)
-    w_c = nt(pick, weights, high)
+    loads[0].wait()
+    loads[1].wait()
+    r_c = rates_v[...]
+    w_c = res_v[...] * jnp.sqrt(r_c)
+    a_c = jnp.exp(-r_c)
+    for s in range(MODES):
+        a_rep[s] = jnp.broadcast_to(a_c[s : s + 1], (CHUNKS, chans))
+        w_rep[s] = jnp.broadcast_to(w_c[s : s + 1], (CHUNKS, chans))
 
     first = lax.broadcasted_iota(jnp.int32, (CHUNKS, chans), 0) == 0
     tail = CHUNKS * (blocks - 2)
 
+    loads[2].wait()
+
     def short(which, source):
-        loads[which].wait()
+        loads[3 + which].wait()
         laid = nt(perm[...], source[...])
         m = (1, 2, 0)[which]
-        tap = [taps_ref[3 * m + j : 3 * m + j + 1, :] for j in range(3)]
+        tap = [taps_v[3 * m + j : 3 * m + j + 1, :] for j in range(3)]
         ext[2 * CHUNKS :, :] = laid
         for n in range(2):
             block = laid[tail + n * CHUNKS : tail + (n + 1) * CHUNKS]
@@ -329,6 +332,7 @@
             device_id_type=MESH,
         ).wait_recv()
 
+    loads[6].wait()
     k8 = lax.broadcasted_iota(jnp.int32, (CHUNKS, LANES), 0).astype(F32) * float(blocks)
     for h in range(halves):
         lanes = slice(h * LANES, (h + 1) * LANES)
@@ -341,7 +345,7 @@
             ]
         )
         start = w_rep[:, :, lanes] * a * (lead + cin[:, :, lanes])
-        gain = gain_ref[:, lanes]
+        gain = gain_v[:, lanes]
 
         def finish(i, state):
             rows = pl.ds(pl.multiple_of(i * CHUNKS, CHUNKS), CHUNKS)
@@ -362,7 +366,7 @@
                 forward(way, 1, h, chan)
         share(0, h, chan)
 
-    loads[3].wait()
+    loads[7].wait()
 
     def product(c):
         cols = pl.ds(pl.multiple_of(c * chans, chans), chans)
@@ -415,9 +419,13 @@
     return pl.pallas_call(
         functools.partial(kernel, nseq, nchan),
         out_shape=jax.ShapeDtypeStruct((weight.shape[0], toks), BF16),
-        in_specs=[anywhere] * 3 + [vmem] * 4 + [anywhere],
+        in_specs=[anywhere] * 8,
         out_specs=vmem,
         scratch_shapes=[
+            pltpu.VMEM(taps.shape, F32),
+            pltpu.VMEM((1, chans), F32),
+            pltpu.VMEM((MODES, chans), F32),
+            pltpu.VMEM((MODES, chans), F32),
             pltpu.VMEM((chans, toks), BF16),
             pltpu.VMEM((chans, toks), BF16),
             pltpu.VMEM((chans, toks), BF16),
@@ -439,7 +447,7 @@
             pltpu.VMEM((MODES, chans), F32),
             pltpu.VMEM((nchan, chans, toks), BF16),
             pltpu.VMEM((weight.shape[0], toks), F32),
-            dma((4,)),
+            dma((8,)),
             dma((NZ - 1,)),
             dma((NZ - 1,)),
             dma((max(nx - 1, 1),)),
@@ -452,10 +460,10 @@
             dma((1 + 2 * half, 2)),
         ],
         compiler_params=pltpu.CompilerParams(
-            collective_id=0, has_side_effects=True, vmem_limit_bytes=40 * 1024 * 1024
+            collective_id=0, has_side_effects=True, vmem_limit_bytes=62 * 1024 * 1024
         ),
         name="hyena",
-    )(gate, key, value, taps, gain.reshape(1, -1), rates, residues, weight)
+    )(gate, key, value, taps, gain.reshape(1, -1), rates.T, residues.T, weight)
 
 
 def solution(mesh):

time: 52.4 us -> 46 us (0.88)
  local copies, waits for them, and re-layouts: 7.98 us -> 1.57 us
    unnamed x15 -> x1, local copies, waits for them, and re-layouts: 7.98 us -> 1.57 us
where the time goes in v2:
time: 46 us; the launch traced here: 45.8 us
  Pallas kernels  44.2 us (96%)
  local copies, waits for them, and re-layouts  1.57 us (3%)
    pallas_call x1, Pallas kernels, body(): pl.pallas_call(functools.partial(kernel, nseq, nchan), out_shape=jax.Shap...  44.2 us
    unnamed x1, local copies, waits for them, and re-layouts  1.57 us

profile of v2, /device:TPU:1, one launch (start us, length us, event | category | flops | bytes accessed | tf_op | source)
XLA Modules:
  0.0 45.8 jit_solution(2407160248443045977)
XLA Ops:
  0.0 44.2 %hyena.1 = bf16[256,256]{1,0:T(8,128)(2,1)} custom-call(bf16[256,256]{1,0:T(8,128)(2,1)} %gate_hbm.1, bf16[256,256]{1,0:T(8,128)(2,1)} %key_hbm.1, bf16[256,256]{1,0:T(8,128)(2,1)} %value_hbm.1, f32[9,256]{1,0:T(8,128)} %taps_hbm.1, f32[1,256]{1,0:T(1,128)} %bitcast.5, f32[16,256]{1,0:T(8,128)} %bitcast.3, f32[16,256]{1,0:T(8,128)} %bitcast.4, ...), custom_call_target="tpu_custom_call" | custom-call | tf_op jit(solution)/shard_map/hyena/pallas_call | solution.py:419
  44.3 1.6 %copy.10 = bf16[256,256]{1,0:T(8,128)(2,1)} copy(bf16[256,256]{1,0:T(8,128)(2,1)} %hyena.1) | data formatting | bytes 262144

commit v3 on v2

v3 whole, which is shorter than its diff:
```python
import functools
import math

import jax
import jax.numpy as jnp
from jax import lax
from jax.experimental import pallas as pl
from jax.experimental.pallas import tpu as pltpu
from jax.sharding import PartitionSpec as P

MESH = pl.DeviceIdType.MESH
F32 = jnp.float32
BF16 = jnp.bfloat16
NZ = 8
MODES = 16
CHUNKS = 8
LANES = 128
MSG = 32
LATE = 24


def rounded(value):
    return value.astype(BF16).astype(F32)


def nt(lhs, rhs):
    return lax.dot_general(lhs, rhs, (((1,), (1,)), ((), ())), preferred_element_type=F32)


def kernel(
    nseq,
    nchan,
    gate_hbm,
    key_hbm,
    value_hbm,
    taps_hbm,
    gain_hbm,
    rates_hbm,
    res_hbm,
    weight_hbm,
    out_ref,
    taps_v,
    gain_v,
    rates_v,
    res_v,
    gate_v,
    key_v,
    value_v,
    weight_v,
    perm,
    ext,
    u_ref,
    gs_ref,
    y_ref,
    cin,
    zbuf,
    xbuf,
    tmsg,
    carry,
    edge,
    w_v,
    a_own,
    lead_own,
    states,
    early,
    modes,
    late,
    a_rep,
    lead_rep,
    gathered,
    acc,
    other_acc,
    in_sem,
    z_s,
    z_r,
    x_s,
    x_r,
    early_s,
    early_r,
    late_s,
    late_r,
    own_w,
    sib_s,
    sib_r,
    sum_s,
    sum_r,
    hello_sem,
):
    nx = nseq // NZ
    ny = nchan // 2
    half = ny // 2
    toks = gate_v.shape[1]
    chans = gate_v.shape[0]
    blocks = toks // CHUNKS
    halves = chans // LANES
    seq = lax.axis_index("seq")
    chan = lax.axis_index("chan")
    x, z = seq // NZ, seq % NZ
    y, core = chan // 2, chan % 2
    sibling = chan + 1 - 2 * core

    loads = []
    for n, (src, dst) in enumerate(
        (
            (rates_hbm, rates_v),
            (res_hbm, res_v),
            (taps_hbm, taps_v),
            (key_hbm, key_v),
            (value_hbm, value_v),
            (gate_hbm, gate_v),
            (gain_hbm, gain_v),
        )
    ):
        copy = pltpu.make_async_copy(src, dst, in_sem.at[n])
        copy.start()
        loads.append(copy)

    rows_w = weight_hbm.shape[0]

    def columns(b, of):
        return weight_hbm.at[:, pl.ds(pl.multiple_of((2 * b + of) * chans, chans), chans)]

    def held(b, of):
        return weight_v.at[pl.ds(of * rows_w, rows_w), pl.ds(b * chans, chans)]

    own_weights = [pltpu.make_async_copy(columns(b, core), held(b, 0), own_w.at[b]) for b in range(ny)]
    for copy in own_weights:
        copy.start()

    def along_y(d):
        return ((y + d + ny) % ny) * 2 + core

    def along_z(d):
        return x * NZ + (z + d) % NZ

    barrier = pltpu.get_barrier_semaphore()

    def greet(peer):
        pl.semaphore_signal(barrier, inc=1, device_id=peer, device_id_type=MESH)

    ring = [(dist, 1, dist + 1) for dist in range(half)]
    steps = [(0, 2, 2), (0, 1, 1), (2, 2, 4), (2, 1, 3)] if half == 4 else ring
    near = sorted({way * hop % ny for _, hop, _ in ring + steps for way in (1, -1)})
    for d in near:
        greet((seq, along_y(d)))
    greet((seq, sibling))
    for d in range(1, NZ):
        pl.when(z + d < NZ)(functools.partial(greet, (seq + d, chan)))
    for d in range(1, nx):
        pl.when(x >= d)(functools.partial(greet, (seq - d * NZ, chan)))

    def send(src, dst, ssem, rsem, peer):
        pltpu.make_async_remote_copy(
            src_ref=src,
            dst_ref=dst,
            send_sem=ssem,
            recv_sem=rsem,
            device_id=peer,
            device_id_type=MESH,
        ).start()

    def landing(ref, ssem, rsem):
        return pltpu.make_async_remote_copy(
            src_ref=ref,
            dst_ref=ref,
            send_sem=ssem,
            recv_sem=rsem,
            device_id=(seq, chan),
            device_id_type=MESH,
        )

    def landed(ref, rsem):
        landing(ref, in_sem.at[0], rsem).wait_recv()

    def left(ref, ssem):
        landing(ref, ssem, in_sem.at[0]).wait_send()

    row = lax.broadcasted_iota(jnp.int32, (toks, toks), 0)
    col = lax.broadcasted_iota(jnp.int32, (toks, toks), 1)
    perm[...] = jnp.where(col == (row % CHUNKS) * blocks + row // CHUNKS, 1.0, 0.0).astype(BF16)
    k8 = lax.broadcasted_iota(jnp.int32, (CHUNKS, chans), 0).astype(F32) * float(blocks) + 1.0
    loads[0].wait()
    loads[1].wait()
    r_c = rates_v[...]
    w_c = res_v[...] * jnp.sqrt(r_c)
    w_v[...] = w_c
    modes[y, 0:MODES, :] = r_c[:, 0:LANES]
    modes[y, MODES:, :] = w_c[:, 0:LANES]
    for s in range(MODES):
        a_own[s] = jnp.exp(-jnp.broadcast_to(rates_v[s : s + 1, :], (CHUNKS, chans)))

    def leads(b):
        for s in range(MODES):
            rate = jnp.broadcast_to(modes[b, s : s + 1, :], (CHUNKS, LANES))
            weight = jnp.broadcast_to(modes[b, MODES + s : MODES + s + 1, :], (CHUNKS, LANES))
            a_rep[b, s] = jnp.exp(-rate)
            lead_rep[b, s] = weight * jnp.exp(-rate * k8[:, 0:LANES])

    at_k0 = lax.broadcasted_iota(jnp.int32, (CHUNKS, chans), 0) == 0
    tail = CHUNKS * (blocks - 2)
    loads[2].wait()

    def taps_of(m):
        return [taps_v[3 * m + j : 3 * m + j + 1, :] for j in range(3)]

    def short(m, source):
        laid = nt(perm[...], source[...])
        tap = taps_of(m)
        ext[2 * CHUNKS :, :] = laid
        for n in range(2):
            block = laid[tail + n * CHUNKS : tail + (n + 1) * CHUNKS]
            ext[n * CHUNKS : (n + 1) * CHUNKS, :] = jnp.where(at_k0, 0.0, pltpu.roll(block, 1, 0))
        result = tap[0] * laid
        result = result + tap[1] * ext[CHUNKS : CHUNKS + toks, :]
        result = result + tap[2] * ext[0:toks, :]
        last = laid[toks - 1 : toks]
        prev = laid[toks - 1 - CHUNKS : toks - CHUNKS]
        return result, tap[1] * last + tap[2] * prev, tap[2] * last

    own = zbuf.at[z]
    own[24:MSG, :] = jnp.zeros((MSG - 24, chans), F32)
    loads[3].wait()
    key_short, q0, q1 = short(1, key_v)
    own[16:17, :] = key_short[0:1]
    own[17:18, :] = key_short[CHUNKS : CHUNKS + 1]
    own[20:21, :] = q0
    own[21:22, :] = q1
    loads[4].wait()
    value_short, q0, q1 = short(2, value_v)
    own[18:19, :] = value_short[0:1]
    own[19:20, :] = value_short[CHUNKS : CHUNKS + 1]
    own[22:23, :] = q0
    own[23:24, :] = q1
    u_ref[...] = rounded(key_short * value_short)
    for n in range(2):
        u_ref[n * CHUNKS : n * CHUNKS + 1, :] = jnp.zeros((1, chans), F32)
    loads[5].wait()
    gate_short, q0, q1 = short(0, gate_v)
    own[24:25, :] = q0
    own[25:26, :] = q1

    pl.semaphore_wait(barrier, len(near) + 1 + z + (nx - 1 - x))

    def hello(d):
        pl.semaphore_signal(
            hello_sem.at[d - 1], inc=1, device_id=(seq - d, chan), device_id_type=MESH
        )

    for d in range(1, NZ):
        pl.when(z >= d)(functools.partial(hello, d))

    k3 = lax.broadcasted_iota(jnp.int32, (MODES, CHUNKS, LANES), 1)
    for h in range(halves):
        lanes = slice(h * LANES, (h + 1) * LANES)
        a = a_own[:, :, lanes]

        def scan(i, state):
            u = u_ref[pl.ds(pl.multiple_of(i * CHUNKS, CHUNKS), CHUNKS), lanes]
            return state * a + u[None]

        state = lax.fori_loop(0, blocks, scan, jnp.zeros((MODES, CHUNKS, LANES), F32), unroll=8)
        step = a
        for _ in range(int(math.log2(blocks))):
            step = step * step
        shift = 1
        while shift < CHUNKS:
            moved = jnp.where(k3 >= shift, pltpu.roll(state, shift, 1), 0.0)
            state = state + step * moved
            step = step * step
            shift *= 2
        cin[:, :, lanes] = jnp.where(k3 >= 1, pltpu.roll(state, 1, 1), 0.0)
        for s in range(MODES):
            own[s : s + 1, lanes] = state[s, CHUNKS - 1 : CHUNKS, :]

    def send_state(d):
        send(own, own, z_s.at[d - 1], z_r.at[d - 1], (along_z(d), chan))

    for d in range(1, NZ):
        pl.when(z + d >= NZ)(functools.partial(send_state, d))

    def origin(way, dist):
        return (y + (2 * way - 1) * dist + ny) % ny

    def pass_on(gather, way, src, item):
        routes, parts, side, ssem, rsem = gather
        for at, hop, dist in routes:
            if at == src and (dist < half or way == side(item)):
                for ref, n in parts(origin(way, src), item):
                    sem = (way, dist - 1, n)
                    send(ref, ref, ssem.at[sem], rsem.at[sem], (seq, along_y((1 - 2 * way) * hop)))

    def arrive(gather, dist, items):
        _, parts, side, _, rsem = gather
        for item in items:
            for way in range(2):
                if dist < half or way == side(item):
                    for ref, n in parts(origin(way, dist), item):
                        landed(ref, rsem.at[way, dist - 1, n])
                    pass_on(gather, way, dist, item)

    def all_left(gather, items):
        routes, parts, side, ssem, _ = gather
        for _, _, dist in routes:
            for item in items:
                for way in range(2):
                    if dist < half or way == side(item):
                        for ref, n in parts(y, item):
                            left(ref, ssem.at[way, dist - 1, n])

    GATE, LOCAL = 0, 1

    def early_parts(b, item):
        if item == GATE:
            return (modes.at[b], 2), (early.at[GATE, b], GATE)
        return ((early.at[LOCAL, b], LOCAL),)

    first = (ring, early_parts, lambda item: item, early_s, early_r)

    early[GATE, y] = gate_short[:, 0:LANES].astype(BF16)
    gs_ref[...] = gate_short[:, LANES:]
    for way in range(2):
        pass_on(first, way, 0, GATE)

    loads[6].wait()
    for h in range(halves):
        lanes = slice(h * LANES, (h + 1) * LANES)
        a = a_own[:, :, lanes]
        w = jnp.stack([jnp.broadcast_to(w_v[s : s + 1, lanes], (CHUNKS, LANES)) for s in range(MODES)])
        gain = gain_v[:, lanes]

        def local(i, state):
            both = []
            for n in range(2):
                rows = pl.ds(pl.multiple_of((2 * i + n) * CHUNKS, CHUNKS), CHUNKS)
                u = u_ref[rows, lanes]
                state = state * a + u[None]
                both.append(jnp.sum(state * w, axis=0) + gain * u)
            rows = pl.ds(pl.multiple_of(i * 2 * CHUNKS, 2 * CHUNKS), 2 * CHUNKS)
            if h == 0:
                early[LOCAL, y, rows, :] = jnp.concatenate(both).astype(BF16)
            else:
                y_ref[rows, :] = jnp.concatenate(both)
            return state

        lax.fori_loop(0, blocks // 2, local, cin[:, :, lanes], unroll=2)
        if h == 0:
            for way in range(2):
                pass_on(first, way, 0, LOCAL)
    for s in range(MODES):
        rate = jnp.broadcast_to(rates_v[s : s + 1, :], (CHUNKS, chans))
        lead_own[s] = jnp.broadcast_to(w_v[s : s + 1, :], (CHUNKS, chans)) * jnp.exp(-rate * k8)

    for b in range(ny):
        send(columns(b, 1 - core), held(b, 1), sib_s.at[b], sib_r.at[b], (seq, sibling))

    def gather_first(dists):
        for dist in dists:
            arrive(first, dist, (GATE, LOCAL))
            for way in range(2 if dist < half else 1):
                leads(origin(way, dist))

    gather_first(range(1, min(half, 3)))

    def decay(count):
        return jnp.exp(-r_c * count)

    def edge_tokens(q, msg):
        u0 = rounded((msg[16:17] + q[0:1]) * (msg[18:19] + q[2:3]))
        u1 = rounded((msg[17:18] + q[1:2]) * (msg[19:20] + q[3:4]))
        return u0, u1

    span = float(toks)
    d0, d1, d2 = decay(span), decay(span - 1.0), decay(span - 2.0)
    e0, e1, e2 = decay(NZ * span), decay(NZ * span - 1.0), decay(NZ * span - 2.0)

    def state_of(d):
        landed(zbuf.at[(z + d) % NZ], z_r.at[NZ - d - 1])

    def send_higher(d):
        pl.semaphore_wait(hello_sem.at[d - 1], 1)
        send_state(d)

    for d in range(1, NZ):
        pl.when(z + d < NZ)(functools.partial(send_higher, d))
    for d in range(1, NZ):
        state_of(d)
    msg = zbuf[0]
    cur, q = msg[:MODES], msg[20:26]
    mine, mine_q = jnp.zeros((MODES, chans), F32), jnp.zeros((6, chans), F32)
    for n in range(1, NZ):
        here = z == n
        mine = jnp.where(here, cur, mine)
        mine_q = jnp.where(here, q, mine_q)
        msg = zbuf[n]
        u0, u1 = edge_tokens(q, msg)
        cur = d0 * cur + msg[:MODES] + d1 * u0 + d2 * u1
        q = msg[20:26]
    tmsg[0:MODES, :] = cur
    tmsg[16:20, :] = zbuf[0, 16:20, :]
    tmsg[20:26, :] = q
    tmsg[26:MSG, :] = jnp.zeros((MSG - 26, chans), F32)

    def send_total(d):
        send(tmsg, xbuf.at[x], x_s.at[d - 1], x_r.at[d - 1], (seq + d * NZ, chan))

    for d in range(1, nx):
        pl.when(x + d < nx)(functools.partial(send_total, d))

    gather_first(range(3, half))

    carry[...] = jnp.zeros_like(carry)
    edge[...] = jnp.zeros_like(edge)

    def fold(n):
        landed(xbuf.at[n], x_r.at[x - n - 1])
        msg = xbuf[n]
        u0, u1 = edge_tokens(edge[0:6, :], msg)
        carry[...] = e0 * carry[...] + msg[:MODES] + e1 * u0 + e2 * u1
        edge[0:6, :] = msg[20:26]

    for n in range(nx - 1):
        pl.when(n < x)(functools.partial(fold, n))
    cur, q = carry[...], edge[0:6, :]
    u0, u1 = edge_tokens(q, zbuf[0])
    ahead = z.astype(F32) * span
    inside = mine + decay(ahead) * cur + decay(ahead - 1.0) * u0 + decay(ahead - 2.0) * u1
    at_first = z == 0
    state_in = jnp.where(at_first, cur, inside)
    q = jnp.where(at_first, q, mine_q)
    u0, u1 = edge_tokens(q, own[...])
    back = jnp.exp(r_c)
    gain = gain_v[...]
    states[0:MODES, :] = state_in + back * u0 + back * back * u1
    states[16:17, :] = gain * u0 - jnp.sum(w_c * back, axis=0, keepdims=True) * u1
    states[17:18, :] = gain * u1
    states[18:20, :] = q[4:6]
    states[20:LATE, :] = jnp.zeros((LATE - 20, chans), F32)
    late[y] = states[:, 0:LANES]

    top = lax.broadcasted_iota(jnp.int32, (CHUNKS, LANES), 0) == 0

    def rebuild(a, lead, found, conv_of, gate_of, dst, exact):
        start = jnp.stack(
            [jnp.broadcast_to(found(s), (CHUNKS, LANES)) * lead(s) for s in range(MODES)]
        )
        edges = [found(MODES + n) for n in range(4)]

        def finish(i, state, first_rows=False):
            rows = pl.ds(pl.multiple_of(i * 2 * CHUNKS, 2 * CHUNKS), 2 * CHUNKS)
            conv, gate = conv_of(rows).astype(F32), gate_of(rows).astype(F32)
            both = []
            for n in range(2):
                part = slice(n * CHUNKS, (n + 1) * CHUNKS)
                total, scale = conv[part] + jnp.sum(state, axis=0), gate[part]
                if first_rows:
                    total = total + jnp.where(top, edges[n], 0.0)
                    scale = scale + jnp.where(top, edges[2 + n], 0.0)
                both.append(scale * (rounded(total) if exact else total))
                state = state * a
            dst(rows, jnp.concatenate(both).astype(BF16))
            return state

        lax.fori_loop(1, blocks // 2, finish, finish(0, start, True), unroll=3)

    def store(b, lanes):
        def put(rows, value):
            gathered[b, rows, lanes] = value

        return put

    whole = slice(LANES, 2 * LANES)
    rebuild(
        a_own[:, :, whole],
        lambda s: lead_own[s, :, whole],
        lambda s: states[s : s + 1, whole],
        lambda rows: y_ref[rows, :],
        lambda rows: gs_ref[rows, :],
        store(y, whole),
        True,
    )

    pieces = toks // 2

    def late_parts(b, item):
        if item == 0:
            return ((late.at[b], 0),)
        rows = pl.ds((item - 1) * pieces, pieces)
        return ((gathered.at[b, rows, pl.ds(LANES, LANES)], item),)

    second = (steps, late_parts, lambda item: item // 2, late_s, late_r)
    for item in range(3):
        for way in range(2):
            pass_on(second, way, 0, item)

    def slots(dist):
        return sorted({dist, ny - dist}) if dist else [0]

    def first_half(dist):
        for d in slots(dist):
            b = (y + d) % ny
            rebuild(
                a_rep[b] if d else a_own[:, :, 0:LANES],
                (lambda s: lead_rep[b, s]) if d else (lambda s: lead_own[s, :, 0:LANES]),
                lambda s: late[b, s : s + 1, :],
                lambda rows: early[LOCAL, b, rows, :],
                lambda rows: early[GATE, b, rows, :],
                store(b, slice(0, LANES)),
                False,
            )

    def product(dists, of):
        total = None
        for dist in dists:
            for d in slots(dist):
                b = (y + d) % ny
                cols = pl.ds(pl.multiple_of(b * chans, chans), chans)
                term = nt(weight_v[of * rows_w : (of + 1) * rows_w, cols], gathered[b])
                total = term if total is None else total + term
        return total

    def add(dists):
        for of in range(2):
            acc[of] += product(dists, of)

    for b in range(ny):
        own_weights[b].wait()
        landed(held(b, 1), sib_r.at[b])
    first_half(0)
    for of in range(2):
        acc[of] = product([0], of)
    if half == 4:
        arrive(second, 2, (0,))
        first_half(2)
        arrive(second, 2, (1, 2))
        arrive(second, 1, (0,))
        first_half(1)
        arrive(second, 1, (1, 2))
        add([1, 2])
        arrive(second, 3, (0,))
        first_half(3)
        gather_first([4])
        arrive(second, 4, (0,))
        first_half(4)
        arrive(second, 4, (1, 2))
        arrive(second, 3, (1, 2))
        last = [3, 4]
    else:
        gather_first([half])
        for dist in range(1, half + 1):
            arrive(second, dist, (0, 1, 2))
            first_half(dist)
        last = list(range(1, half + 1))
    acc[1] += product(last, 1)
    send(acc.at[1], other_acc, sum_s.at[0], sum_r.at[0], (seq, sibling))
    acc[0] += product(last, 0)
    landed(other_acc, sum_r.at[0])
    acc[0] += other_acc[...]
    out_ref[...] = jnp.dot(acc[0].astype(BF16), perm[...], preferred_element_type=F32).astype(BF16)

    for d in range(1, NZ):
        left(own, z_s.at[d - 1])
    for d in range(1, nx):
        pl.when(x + d < nx)(functools.partial(left, tmsg, x_s.at[d - 1]))
    all_left(first, (GATE, LOCAL))
    all_left(second, (0, 1, 2))
    for b in range(ny):
        left(columns(b, 1 - core), sib_s.at[b])
    left(acc.at[1], sum_s.at[0])


def body(nseq, nchan, gate, key, value, taps, gain, rates, residues, weight):
    chans, toks = gate.shape
    nx, ny = nseq // NZ, nchan // 2
    vmem = pl.BlockSpec(memory_space=pltpu.VMEM)
    anywhere = pl.BlockSpec(memory_space=pl.ANY)
    dma = pltpu.SemaphoreType.DMA
    return pl.pallas_call(
        functools.partial(kernel, nseq, nchan),
        out_shape=jax.ShapeDtypeStruct((weight.shape[0], toks), BF16),
        in_specs=[anywhere] * 8,
        out_specs=vmem,
        scratch_shapes=[
            pltpu.VMEM(taps.shape, F32),
            pltpu.VMEM((1, chans), F32),
            pltpu.VMEM((MODES, chans), F32),
            pltpu.VMEM((MODES, chans), F32),
            pltpu.VMEM((chans, toks), BF16),
            pltpu.VMEM((chans, toks), BF16),
            pltpu.VMEM((chans, toks), BF16),
            pltpu.VMEM((2 * weight.shape[0], weight.shape[1] // 2), BF16),
            pltpu.VMEM((toks, toks), BF16),
            pltpu.VMEM((toks + 2 * CHUNKS, chans), F32),
            pltpu.VMEM((toks, chans), F32),
            pltpu.VMEM((toks, LANES), F32),
            pltpu.VMEM((toks, LANES), F32),
            pltpu.VMEM((MODES, CHUNKS, chans), F32),
            pltpu.VMEM((NZ, MSG, chans), F32),
            pltpu.VMEM((nx, MSG, chans), F32),
            pltpu.VMEM((MSG, chans), F32),
            pltpu.VMEM((MODES, chans), F32),
            pltpu.VMEM((8, chans), F32),
            pltpu.VMEM((MODES, chans), F32),
            pltpu.VMEM((MODES, CHUNKS, chans), F32),
            pltpu.VMEM((MODES, CHUNKS, chans), F32),
            pltpu.VMEM((LATE, chans), F32),
            pltpu.VMEM((2, ny, toks, LANES), BF16),
            pltpu.VMEM((ny, 2 * MODES, LANES), F32),
            pltpu.VMEM((ny, LATE, LANES), F32),
            pltpu.VMEM((ny, MODES, CHUNKS, LANES), F32),
            pltpu.VMEM((ny, MODES, CHUNKS, LANES), F32),
            pltpu.VMEM((ny, toks, chans), BF16),
            pltpu.VMEM((2, weight.shape[0], toks), F32),
            pltpu.VMEM((weight.shape[0], toks), F32),
            dma((7,)),
            dma((NZ - 1,)),
            dma((NZ - 1,)),
            dma((max(nx - 1, 1),)),
            dma((max(nx - 1, 1),)),
            dma((2, ny // 2, 3)),
            dma((2, ny // 2, 3)),
            dma((2, ny // 2, 3)),
            dma((2, ny // 2, 3)),
            dma((ny,)),
            dma((ny,)),
            dma((ny,)),
            dma((1,)),
            dma((1,)),
            pltpu.SemaphoreType.REGULAR((NZ - 1,)),
        ],
        compiler_params=pltpu.CompilerParams(
            collective_id=0, has_side_effects=True, vmem_limit_bytes=62 * 1024 * 1024
        ),
        name="hyena",
    )(gate, key, value, taps, gain.reshape(1, -1), rates.T, residues.T, weight)


def solution(mesh):
    in_specs = (
        P("chan", "seq"),
        P("chan", "seq"),
        P("chan", "seq"),
        P(None, "chan"),
        P("chan"),
        P("chan", None),
        P("chan", None),
        P("chan", None),
    )
    return jax.shard_map(
        functools.partial(body, mesh.shape["seq"], mesh.shape["chan"]),
        mesh=mesh,
        in_specs=in_specs,
        out_specs=P("chan", "seq"),
        check_vma=False,
    )
```

time: 46 us -> 41.5 us (0.902)
  Pallas kernels: 44.2 us -> 39.5 us
    pallas_call x1, Pallas kernels: 44.2 us -> 39.5 us  [body(): pl.pallas_call(functools.partial(kernel, nseq, nchan), out_shape=jax.Shap...]
where the time goes in v3:
time: 41.5 us; the launch traced here: 41.1 us
  Pallas kernels  39.5 us (95%)
  local copies, waits for them, and re-layouts  1.57 us (4%)
    pallas_call x1, Pallas kernels, body(): pl.pallas_call(functools.partial(kernel, nseq, nchan), out_shape=jax.Shap...  39.5 us
    unnamed x1, local copies, waits for them, and re-layouts  1.57 us

profile of v3, /device:TPU:1, one launch (start us, length us, event | category | flops | bytes accessed | tf_op | source)
XLA Modules:
  0.0 41.1 jit_solution(12713915038882484236)
XLA Ops:
  0.0 39.5 %hyena.1 = bf16[256,256]{1,0:T(8,128)(2,1)} custom-call(bf16[256,256]{1,0:T(8,128)(2,1)} %gate_hbm.1, bf16[256,256]{1,0:T(8,128)(2,1)} %key_hbm.1, bf16[256,256]{1,0:T(8,128)(2,1)} %value_hbm.1, f32[9,256]{1,0:T(8,128)} %taps_hbm.1, f32[1,256]{1,0:T(1,128)} %bitcast.5, f32[16,256]{1,0:T(8,128)} %bitcast.3, f32[16,256]{1,0:T(8,128)} %bitcast.4, ...), custom_call_target="tpu_custom_call" | custom-call | tf_op jit(solution)/shard_map/hyena/pallas_call | solution.py:577
  39.5 1.6 %copy.10 = bf16[256,256]{1,0:T(8,128)(2,1)} copy(bf16[256,256]{1,0:T(8,128)(2,1)} %hyena.1) | data formatting | bytes 262144

commit v4 on v3

--- a/solution.py
+++ b/solution.py
@@ -235,9 +235,10 @@
     for n in range(2):
         u_ref[n * CHUNKS : n * CHUNKS + 1, :] = jnp.zeros((1, chans), F32)
     loads[5].wait()
-    gate_short, q0, q1 = short(0, gate_v)
-    own[24:25, :] = q0
-    own[25:26, :] = q1
+    gate_tap = taps_of(0)
+    gate_end = nt(perm[tail:, :], gate_v[...])
+    own[24:25, :] = gate_tap[1] * gate_end[15:16] + gate_tap[2] * gate_end[7:8]
+    own[25:26, :] = gate_tap[2] * gate_end[15:16]
 
     pl.semaphore_wait(barrier, len(near) + 1 + z + (nx - 1 - x))
 
@@ -281,10 +282,10 @@
     def origin(way, dist):
         return (y + (2 * way - 1) * dist + ny) % ny
 
-    def pass_on(gather, way, src, item):
+    def pass_on(gather, way, src, item, to=None):
         routes, parts, side, ssem, rsem = gather
         for at, hop, dist in routes:
-            if at == src and (dist < half or way == side(item)):
+            if at == src and (dist < half or way == side(item)) and to in (None, dist):
                 for ref, n in parts(origin(way, src), item):
                     sem = (way, dist - 1, n)
                     send(ref, ref, ssem.at[sem], rsem.at[sem], (seq, along_y((1 - 2 * way) * hop)))
@@ -316,6 +317,7 @@
 
     first = (ring, early_parts, lambda item: item, early_s, early_r)
 
+    gate_short, _, _ = short(0, gate_v)
     early[GATE, y] = gate_short[:, 0:LANES].astype(BF16)
     gs_ref[...] = gate_short[:, LANES:]
     for way in range(2):
@@ -369,77 +371,9 @@
         u1 = rounded((msg[17:18] + q[1:2]) * (msg[19:20] + q[3:4]))
         return u0, u1
 
-    span = float(toks)
-    d0, d1, d2 = decay(span), decay(span - 1.0), decay(span - 2.0)
-    e0, e1, e2 = decay(NZ * span), decay(NZ * span - 1.0), decay(NZ * span - 2.0)
-
-    def state_of(d):
-        landed(zbuf.at[(z + d) % NZ], z_r.at[NZ - d - 1])
-
-    def send_higher(d):
-        pl.semaphore_wait(hello_sem.at[d - 1], 1)
-        send_state(d)
-
-    for d in range(1, NZ):
-        pl.when(z + d < NZ)(functools.partial(send_higher, d))
-    for d in range(1, NZ):
-        state_of(d)
-    msg = zbuf[0]
-    cur, q = msg[:MODES], msg[20:26]
-    mine, mine_q = jnp.zeros((MODES, chans), F32), jnp.zeros((6, chans), F32)
-    for n in range(1, NZ):
-        here = z == n
-        mine = jnp.where(here, cur, mine)
-        mine_q = jnp.where(here, q, mine_q)
-        msg = zbuf[n]
-        u0, u1 = edge_tokens(q, msg)
-        cur = d0 * cur + msg[:MODES] + d1 * u0 + d2 * u1
-        q = msg[20:26]
-    tmsg[0:MODES, :] = cur
-    tmsg[16:20, :] = zbuf[0, 16:20, :]
-    tmsg[20:26, :] = q
-    tmsg[26:MSG, :] = jnp.zeros((MSG - 26, chans), F32)
-
-    def send_total(d):
-        send(tmsg, xbuf.at[x], x_s.at[d - 1], x_r.at[d - 1], (seq + d * NZ, chan))
-
-    for d in range(1, nx):
-        pl.when(x + d < nx)(functools.partial(send_total, d))
-
-    gather_first(range(3, half))
-
-    carry[...] = jnp.zeros_like(carry)
-    edge[...] = jnp.zeros_like(edge)
-
-    def fold(n):
-        landed(xbuf.at[n], x_r.at[x - n - 1])
-        msg = xbuf[n]
-        u0, u1 = edge_tokens(edge[0:6, :], msg)
-        carry[...] = e0 * carry[...] + msg[:MODES] + e1 * u0 + e2 * u1
-        edge[0:6, :] = msg[20:26]
-
-    for n in range(nx - 1):
-        pl.when(n < x)(functools.partial(fold, n))
-    cur, q = carry[...], edge[0:6, :]
-    u0, u1 = edge_tokens(q, zbuf[0])
-    ahead = z.astype(F32) * span
-    inside = mine + decay(ahead) * cur + decay(ahead - 1.0) * u0 + decay(ahead - 2.0) * u1
-    at_first = z == 0
-    state_in = jnp.where(at_first, cur, inside)
-    q = jnp.where(at_first, q, mine_q)
-    u0, u1 = edge_tokens(q, own[...])
-    back = jnp.exp(r_c)
-    gain = gain_v[...]
-    states[0:MODES, :] = state_in + back * u0 + back * back * u1
-    states[16:17, :] = gain * u0 - jnp.sum(w_c * back, axis=0, keepdims=True) * u1
-    states[17:18, :] = gain * u1
-    states[18:20, :] = q[4:6]
-    states[20:LATE, :] = jnp.zeros((LATE - 20, chans), F32)
-    late[y] = states[:, 0:LANES]
-
     top = lax.broadcasted_iota(jnp.int32, (CHUNKS, LANES), 0) == 0
 
-    def rebuild(a, lead, found, conv_of, gate_of, dst, exact):
+    def rebuild(a, lead, found, conv_of, gate_of, dst, exact, between=None):
         start = jnp.stack(
             [jnp.broadcast_to(found(s), (CHUNKS, LANES)) * lead(s) for s in range(MODES)]
         )
@@ -460,24 +394,16 @@
             dst(rows, jnp.concatenate(both).astype(BF16))
             return state
 
-        lax.fori_loop(1, blocks // 2, finish, finish(0, start, True), unroll=3)
+        state = lax.fori_loop(1, blocks // 4, finish, finish(0, start, True), unroll=True)
+        if between is not None:
+            between()
+        lax.fori_loop(blocks // 4, blocks // 2, finish, state, unroll=True)
 
     def store(b, lanes):
         def put(rows, value):
             gathered[b, rows, lanes] = value
 
         return put
-
-    whole = slice(LANES, 2 * LANES)
-    rebuild(
-        a_own[:, :, whole],
-        lambda s: lead_own[s, :, whole],
-        lambda s: states[s : s + 1, whole],
-        lambda rows: y_ref[rows, :],
-        lambda rows: gs_ref[rows, :],
-        store(y, whole),
-        True,
-    )
 
     pieces = toks // 2
 
@@ -488,9 +414,109 @@
         return ((gathered.at[b, rows, pl.ds(LANES, LANES)], item),)
 
     second = (steps, late_parts, lambda item: item // 2, late_s, late_r)
-    for item in range(3):
-        for way in range(2):
-            pass_on(second, way, 0, item)
+
+    def launch(state_in, q):
+        u0, u1 = edge_tokens(q, own[...])
+        back = jnp.exp(r_c)
+        gain = gain_v[...]
+        states[0:MODES, :] = state_in + back * u0 + back * back * u1
+        states[16:17, :] = gain * u0 - jnp.sum(w_c * back, axis=0, keepdims=True) * u1
+        states[17:18, :] = gain * u1
+        states[18:20, :] = q[4:6]
+        states[20:LATE, :] = jnp.zeros((LATE - 20, chans), F32)
+        late[y] = states[:, 0:LANES]
+
+        def pass_own(item, to):
+            for way in range(2):
+                pass_on(second, way, 0, item, to)
+
+        far = steps[0][2]
+        pass_own(0, far)
+        whole = slice(LANES, 2 * LANES)
+        rebuild(
+            a_own[:, :, whole],
+            lambda s: lead_own[s, :, whole],
+            lambda s: states[s : s + 1, whole],
+            lambda rows: y_ref[rows, :],
+            lambda rows: gs_ref[rows, :],
+            store(y, whole),
+            True,
+            lambda: pass_own(1, far),
+        )
+
+        pass_own(2, far)
+        if far > 1:
+            for item in range(3):
+                pass_own(item, 1)
+
+    def launch_first():
+        launch(jnp.zeros((MODES, chans), F32), jnp.zeros((6, chans), F32))
+
+    pl.when(seq == 0)(launch_first)
+
+    span = float(toks)
+    d0, d1, d2 = decay(span), decay(span - 1.0), decay(span - 2.0)
+    e0, e1, e2 = decay(NZ * span), decay(NZ * span - 1.0), decay(NZ * span - 2.0)
+
+    def send_higher(d):
+        pl.semaphore_wait(hello_sem.at[d - 1], 1)
+        send_state(d)
+
+    for d in range(1, NZ):
+        pl.when(z + d < NZ)(functools.partial(send_higher, d))
+
+    def state_of(n):
+        landed(zbuf.at[n], z_r.at[(z - n + NZ - 1) % NZ])
+
+    pl.when(z != 0)(functools.partial(state_of, 0))
+    msg = zbuf[0]
+    cur, q = msg[:MODES], msg[20:26]
+    mine, mine_q = jnp.zeros((MODES, chans), F32), jnp.zeros((6, chans), F32)
+    for n in range(1, NZ):
+        here = z == n
+        mine = jnp.where(here, cur, mine)
+        mine_q = jnp.where(here, q, mine_q)
+        pl.when(z != n)(functools.partial(state_of, n))
+        msg = zbuf[n]
+        u0, u1 = edge_tokens(q, msg)
+        cur = d0 * cur + msg[:MODES] + d1 * u0 + d2 * u1
+        q = msg[20:26]
+    tmsg[0:MODES, :] = cur
+    tmsg[16:20, :] = zbuf[0, 16:20, :]
+    tmsg[20:26, :] = q
+    tmsg[26:MSG, :] = jnp.zeros((MSG - 26, chans), F32)
+
+    def send_total(d):
+        send(tmsg, xbuf.at[x], x_s.at[d - 1], x_r.at[d - 1], (seq + d * NZ, chan))
+
+    for d in range(1, nx):
+        pl.when(x + d < nx)(functools.partial(send_total, d))
+
+    gather_first(range(3, half))
+
+    carry[...] = jnp.zeros_like(carry)
+    edge[...] = jnp.zeros_like(edge)
+
+    def fold(n):
+        landed(xbuf.at[n], x_r.at[x - n - 1])
+        msg = xbuf[n]
+        u0, u1 = edge_tokens(edge[0:6, :], msg)
+        carry[...] = e0 * carry[...] + msg[:MODES] + e1 * u0 + e2 * u1
+        edge[0:6, :] = msg[20:26]
+
+    for n in range(nx - 1):
+        pl.when(n < x)(functools.partial(fold, n))
+    def rest():
+        cur, q = carry[...], edge[0:6, :]
+        u0, u1 = edge_tokens(q, zbuf[0])
+        ahead = z.astype(F32) * span
+        inside = mine + decay(ahead) * cur + decay(ahead - 1.0) * u0 + decay(ahead - 2.0) * u1
+        at_first = z == 0
+        state_in = jnp.where(at_first, cur, inside)
+        q = jnp.where(at_first, q, mine_q)
+        launch(state_in, q)
+
+    pl.when(seq > 0)(rest)
 
     def slots(dist):
         return sorted({dist, ny - dist}) if dist else [0]
@@ -529,21 +555,20 @@
     for of in range(2):
         acc[of] = product([0], of)
     if half == 4:
-        arrive(second, 2, (0,))
+        arrive(second, 2, (0, 1, 2))
         first_half(2)
-        arrive(second, 2, (1, 2))
-        arrive(second, 1, (0,))
+        arrive(second, 1, (0, 1, 2))
         first_half(1)
-        arrive(second, 1, (1, 2))
         add([1, 2])
         arrive(second, 3, (0,))
         first_half(3)
         gather_first([4])
         arrive(second, 4, (0,))
         first_half(4)
+        arrive(second, 3, (1, 2))
+        add([3])
         arrive(second, 4, (1, 2))
-        arrive(second, 3, (1, 2))
-        last = [3, 4]
+        last = [4]
     else:
         gather_first([half])
         for dist in range(1, half + 1):
@@ -576,7 +601,7 @@
     dma = pltpu.SemaphoreType.DMA
     return pl.pallas_call(
         functools.partial(kernel, nseq, nchan),
-        out_shape=jax.ShapeDtypeStruct((weight.shape[0], toks), BF16),
+        out_shape=pltpu.VMEM((weight.shape[0], toks), BF16),
         in_specs=[anywhere] * 8,
         out_specs=vmem,
         scratch_shapes=[
@@ -612,8 +637,8 @@
             pltpu.VMEM((2, weight.shape[0], toks), F32),
             pltpu.VMEM((weight.shape[0], toks), F32),
             dma((7,)),
-            dma((NZ - 1,)),
-            dma((NZ - 1,)),
+            dma((max(NZ - 1, 1),)),
+            dma((max(NZ - 1, 1),)),
             dma((max(nx - 1, 1),)),
             dma((max(nx - 1, 1),)),
             dma((2, ny // 2, 3)),
@@ -628,7 +653,7 @@
             pltpu.SemaphoreType.REGULAR((NZ - 1,)),
         ],
         compiler_params=pltpu.CompilerParams(
-            collective_id=0, has_side_effects=True, vmem_limit_bytes=62 * 1024 * 1024
+            collective_id=0, has_side_effects=True, vmem_limit_bytes=60 * 1024 * 1024
         ),
         name="hyena",
     )(gate, key, value, taps, gain.reshape(1, -1), rates.T, residues.T, weight)

time: 41.5 us -> 38.7 us (0.933)
  the two profiles are of different devices: /device:TPU:1 before, /device:TPU:69 now
where the time goes in v4:
time: 38.7 us; the launch traced here: 38.6 us
  Pallas kernels  37.9 us (98%)
  local copies, waits for them, and re-layouts  0.66 us (2%)
    pallas_call x1, Pallas kernels, body(): pl.pallas_call(functools.partial(kernel, nseq, nchan), out_shape=pltpu.VM...  37.9 us

profile of v4, /device:TPU:69, one launch (start us, length us, event | category | flops | bytes accessed | tf_op | source)
XLA Modules:
  0.0 38.6 jit_solution(4402426652697614365)
XLA Ops:
  0.0 37.9 %hyena.1 = bf16[256,256]{1,0:T(8,128)(2,1)S(1)} custom-call(bf16[256,256]{1,0:T(8,128)(2,1)} %gate_hbm.1, bf16[256,256]{1,0:T(8,128)(2,1)} %key_hbm.1, bf16[256,256]{1,0:T(8,128)(2,1)} %value_hbm.1, f32[9,256]{1,0:T(8,128)} %taps_hbm.1, f32[1,256]{1,0:T(1,128)} %bitcast.5, f32[16,256]{1,0:T(8,128)} %bitcast.3, f32[16,256]{1,0:T(8,128)} %bitcast.4, ...), custom_call_target="tpu_custom_call" | custom-call | tf_op jit(solution)/shard_map/hyena/pallas_call | solution.py:602
  37.9 0.7 %copy.10 = bf16[256,256]{1,0:T(8,128)(2,1)} copy(bf16[256,256]{1,0:T(8,128)(2,1)S(1)} %hyena.1) | data formatting | bytes 262144

commit v5 on v4

--- a/solution.py
+++ b/solution.py
@@ -15,7 +15,7 @@
 MODES = 16
 CHUNKS = 8
 LANES = 128
-MSG = 32
+MSG = 24
 LATE = 24
 
 
@@ -57,6 +57,8 @@
     xbuf,
     tmsg,
     carry,
+    last_q,
+    gate_edge,
     edge,
     w_v,
     a_own,
@@ -84,6 +86,8 @@
     sib_r,
     sum_s,
     sum_r,
+    edge_s,
+    edge_r,
     hello_sem,
 ):
     nx = nseq // NZ
@@ -124,9 +128,6 @@
         return weight_v.at[pl.ds(of * rows_w, rows_w), pl.ds(b * chans, chans)]
 
     own_weights = [pltpu.make_async_copy(columns(b, core), held(b, 0), own_w.at[b]) for b in range(ny)]
-    for copy in own_weights:
-        copy.start()
-
     def along_y(d):
         return ((y + d + ny) % ny) * 2 + core
 
@@ -144,6 +145,7 @@
     for d in near:
         greet((seq, along_y(d)))
     greet((seq, sibling))
+    pl.when((z == 0) & (x > 0))(functools.partial(greet, (seq - 1, chan)))
     for d in range(1, NZ):
         pl.when(z + d < NZ)(functools.partial(greet, (seq + d, chan)))
     for d in range(1, nx):
@@ -218,7 +220,6 @@
         return result, tap[1] * last + tap[2] * prev, tap[2] * last
 
     own = zbuf.at[z]
-    own[24:MSG, :] = jnp.zeros((MSG - 24, chans), F32)
     loads[3].wait()
     key_short, q0, q1 = short(1, key_v)
     own[16:17, :] = key_short[0:1]
@@ -234,21 +235,9 @@
     u_ref[...] = rounded(key_short * value_short)
     for n in range(2):
         u_ref[n * CHUNKS : n * CHUNKS + 1, :] = jnp.zeros((1, chans), F32)
-    loads[5].wait()
-    gate_tap = taps_of(0)
-    gate_end = nt(perm[tail:, :], gate_v[...])
-    own[24:25, :] = gate_tap[1] * gate_end[15:16] + gate_tap[2] * gate_end[7:8]
-    own[25:26, :] = gate_tap[2] * gate_end[15:16]
-
-    pl.semaphore_wait(barrier, len(near) + 1 + z + (nx - 1 - x))
-
-    def hello(d):
-        pl.semaphore_signal(
-            hello_sem.at[d - 1], inc=1, device_id=(seq - d, chan), device_id_type=MESH
-        )
-
-    for d in range(1, NZ):
-        pl.when(z >= d)(functools.partial(hello, d))
+
+    follows = jnp.where((z == NZ - 1) & (x < nx - 1), 1, 0)
+    pl.semaphore_wait(barrier, len(near) + 1 + z + (nx - 1 - x) + follows)
 
     k3 = lax.broadcasted_iota(jnp.int32, (MODES, CHUNKS, LANES), 1)
     for h in range(halves):
@@ -276,8 +265,22 @@
     def send_state(d):
         send(own, own, z_s.at[d - 1], z_r.at[d - 1], (along_z(d), chan))
 
+    def send_edge():
+        send(gate_edge, edge, edge_s.at[0], edge_r.at[0], (seq + 1, chan))
+
     for d in range(1, NZ):
         pl.when(z + d >= NZ)(functools.partial(send_state, d))
+
+    def hello(d):
+        pl.semaphore_signal(
+            hello_sem.at[d - 1], inc=1, device_id=(seq - d, chan), device_id_type=MESH
+        )
+
+    for d in range(1, NZ):
+        pl.when(z >= d)(functools.partial(hello, d))
+
+    for copy in own_weights:
+        copy.start()
 
     def origin(way, dist):
         return (y + (2 * way - 1) * dist + ny) % ny
@@ -317,7 +320,12 @@
 
     first = (ring, early_parts, lambda item: item, early_s, early_r)
 
-    gate_short, _, _ = short(0, gate_v)
+    loads[5].wait()
+    gate_short, q0, q1 = short(0, gate_v)
+    gate_edge[0:1, :] = q0
+    gate_edge[1:2, :] = q1
+    gate_edge[2:8, :] = jnp.zeros((6, chans), F32)
+    pl.when((z == NZ - 1) & (x < nx - 1))(send_edge)
     early[GATE, y] = gate_short[:, 0:LANES].astype(BF16)
     gs_ref[...] = gate_short[:, LANES:]
     for way in range(2):
@@ -415,14 +423,16 @@
 
     second = (steps, late_parts, lambda item: item // 2, late_s, late_r)
 
-    def launch(state_in, q):
+    back = jnp.exp(r_c)
+    early_token = jnp.sum(w_c * back, axis=0, keepdims=True)
+
+    def launch(state_in, q, halo):
         u0, u1 = edge_tokens(q, own[...])
-        back = jnp.exp(r_c)
         gain = gain_v[...]
         states[0:MODES, :] = state_in + back * u0 + back * back * u1
-        states[16:17, :] = gain * u0 - jnp.sum(w_c * back, axis=0, keepdims=True) * u1
+        states[16:17, :] = gain * u0 - early_token * u1
         states[17:18, :] = gain * u1
-        states[18:20, :] = q[4:6]
+        states[18:20, :] = halo
         states[20:LATE, :] = jnp.zeros((LATE - 20, chans), F32)
         late[y] = states[:, 0:LANES]
 
@@ -450,17 +460,21 @@
                 pass_own(item, 1)
 
     def launch_first():
-        launch(jnp.zeros((MODES, chans), F32), jnp.zeros((6, chans), F32))
+        launch(jnp.zeros((MODES, chans), F32), jnp.zeros((4, chans), F32), jnp.zeros((2, chans), F32))
 
     pl.when(seq == 0)(launch_first)
 
     span = float(toks)
     d0, d1, d2 = decay(span), decay(span - 1.0), decay(span - 2.0)
+    ahead = z.astype(F32) * span
+    a0, a1, a2 = decay(ahead), decay(ahead - 1.0), decay(ahead - 2.0)
     e0, e1, e2 = decay(NZ * span), decay(NZ * span - 1.0), decay(NZ * span - 2.0)
 
     def send_higher(d):
         pl.semaphore_wait(hello_sem.at[d - 1], 1)
         send_state(d)
+        if d == 1:
+            send_edge()
 
     for d in range(1, NZ):
         pl.when(z + d < NZ)(functools.partial(send_higher, d))
@@ -470,8 +484,8 @@
 
     pl.when(z != 0)(functools.partial(state_of, 0))
     msg = zbuf[0]
-    cur, q = msg[:MODES], msg[20:26]
-    mine, mine_q = jnp.zeros((MODES, chans), F32), jnp.zeros((6, chans), F32)
+    cur, q = msg[:MODES], msg[20:24]
+    mine, mine_q = jnp.zeros((MODES, chans), F32), jnp.zeros((4, chans), F32)
     for n in range(1, NZ):
         here = z == n
         mine = jnp.where(here, cur, mine)
@@ -480,11 +494,10 @@
         msg = zbuf[n]
         u0, u1 = edge_tokens(q, msg)
         cur = d0 * cur + msg[:MODES] + d1 * u0 + d2 * u1
-        q = msg[20:26]
+        q = msg[20:24]
     tmsg[0:MODES, :] = cur
     tmsg[16:20, :] = zbuf[0, 16:20, :]
-    tmsg[20:26, :] = q
-    tmsg[26:MSG, :] = jnp.zeros((MSG - 26, chans), F32)
+    tmsg[20:24, :] = q
 
     def send_total(d):
         send(tmsg, xbuf.at[x], x_s.at[d - 1], x_r.at[d - 1], (seq + d * NZ, chan))
@@ -495,26 +508,26 @@
     gather_first(range(3, half))
 
     carry[...] = jnp.zeros_like(carry)
-    edge[...] = jnp.zeros_like(edge)
+    last_q[...] = jnp.zeros_like(last_q)
 
     def fold(n):
         landed(xbuf.at[n], x_r.at[x - n - 1])
         msg = xbuf[n]
-        u0, u1 = edge_tokens(edge[0:6, :], msg)
+        u0, u1 = edge_tokens(last_q[0:4, :], msg)
         carry[...] = e0 * carry[...] + msg[:MODES] + e1 * u0 + e2 * u1
-        edge[0:6, :] = msg[20:26]
+        last_q[0:4, :] = msg[20:24]
 
     for n in range(nx - 1):
         pl.when(n < x)(functools.partial(fold, n))
     def rest():
-        cur, q = carry[...], edge[0:6, :]
+        cur, q = carry[...], last_q[0:4, :]
         u0, u1 = edge_tokens(q, zbuf[0])
-        ahead = z.astype(F32) * span
-        inside = mine + decay(ahead) * cur + decay(ahead - 1.0) * u0 + decay(ahead - 2.0) * u1
+        inside = mine + a0 * cur + a1 * u0 + a2 * u1
         at_first = z == 0
         state_in = jnp.where(at_first, cur, inside)
         q = jnp.where(at_first, q, mine_q)
-        launch(state_in, q)
+        landed(edge, edge_r.at[0])
+        launch(state_in, q, edge[0:2, :])
 
     pl.when(seq > 0)(rest)
 
@@ -586,6 +599,7 @@
         left(own, z_s.at[d - 1])
     for d in range(1, nx):
         pl.when(x + d < nx)(functools.partial(left, tmsg, x_s.at[d - 1]))
+    pl.when(seq < nseq - 1)(functools.partial(left, gate_edge, edge_s.at[0]))
     all_left(first, (GATE, LOCAL))
     all_left(second, (0, 1, 2))
     for b in range(ny):
@@ -624,6 +638,8 @@
             pltpu.VMEM((MSG, chans), F32),
             pltpu.VMEM((MODES, chans), F32),
             pltpu.VMEM((8, chans), F32),
+            pltpu.VMEM((8, chans), F32),
+            pltpu.VMEM((8, chans), F32),
             pltpu.VMEM((MODES, chans), F32),
             pltpu.VMEM((MODES, CHUNKS, chans), F32),
             pltpu.VMEM((MODES, CHUNKS, chans), F32),
@@ -650,7 +666,9 @@
             dma((ny,)),
             dma((1,)),
             dma((1,)),
-            pltpu.SemaphoreType.REGULAR((NZ - 1,)),
+            dma((1,)),
+            dma((1,)),
+            pltpu.SemaphoreType.REGULAR((max(NZ - 1, 1),)),
         ],
         compiler_params=pltpu.CompilerParams(
             collective_id=0, has_side_effects=True, vmem_limit_bytes=60 * 1024 * 1024

time: 38.7 us -> 38.1 us (0.984)
  the two profiles are of different devices: /device:TPU:69 before, /device:TPU:71 now
where the time goes in v5:
time: 38.1 us; the launch traced here: 38 us
  Pallas kernels  37.3 us (98%)
  local copies, waits for them, and re-layouts  0.66 us (2%)
    pallas_call x1, Pallas kernels, body(): pl.pallas_call(functools.partial(kernel, nseq, nchan), out_shape=pltpu.VM...  37.3 us

profile of v5, /device:TPU:71, one launch (start us, length us, event | category | flops | bytes accessed | tf_op | source)
XLA Modules:
  0.0 38.0 jit_solution(8783003969446899802)
XLA Ops:
  0.0 37.3 %hyena.1 = bf16[256,256]{1,0:T(8,128)(2,1)S(1)} custom-call(bf16[256,256]{1,0:T(8,128)(2,1)} %gate_hbm.1, bf16[256,256]{1,0:T(8,128)(2,1)} %key_hbm.1, bf16[256,256]{1,0:T(8,128)(2,1)} %value_hbm.1, f32[9,256]{1,0:T(8,128)} %taps_hbm.1, f32[1,256]{1,0:T(1,128)} %bitcast.5, f32[16,256]{1,0:T(8,128)} %bitcast.3, f32[16,256]{1,0:T(8,128)} %bitcast.4, ...), custom_call_target="tpu_custom_call" | custom-call | tf_op jit(solution)/shard_map/hyena/pallas_call | solution.py:616
  37.3 0.7 %copy.10 = bf16[256,256]{1,0:T(8,128)(2,1)} copy(bf16[256,256]{1,0:T(8,128)(2,1)S(1)} %hyena.1) | data formatting | bytes 262144

commit v6 on v5

--- a/solution.py
+++ b/solution.py
@@ -268,8 +268,12 @@
     def send_edge():
         send(gate_edge, edge, edge_s.at[0], edge_r.at[0], (seq + 1, chan))
 
-    for d in range(1, NZ):
-        pl.when(z + d >= NZ)(functools.partial(send_state, d))
+    def send_lower(n):
+        d = NZ + n - z
+        send(own, own, z_s.at[d - 1], z_r.at[d - 1], (x * NZ + n, chan))
+
+    for n in sorted(range(NZ - 1), key=lambda n: (n + 2) % 3 + 3 * (n // 3)):
+        pl.when(z > n)(functools.partial(send_lower, n))
 
     def hello(d):
         pl.semaphore_signal(

time: 38.1 us -> 37.9 us (level)
  the two profiles are of different devices: /device:TPU:71 before, /device:TPU:5 now
where the time goes in v6:
time: 37.9 us; the launch traced here: 37.7 us
  Pallas kernels  37 us (98%)
  local copies, waits for them, and re-layouts  0.66 us (2%)
    pallas_call x1, Pallas kernels, body(): pl.pallas_call(functools.partial(kernel, nseq, nchan), out_shape=pltpu.VM...  37 us

profile of v6, /device:TPU:5, one launch (start us, length us, event | category | flops | bytes accessed | tf_op | source)
XLA Modules:
  0.0 37.7 jit_solution(16860903395960310113)
XLA Ops:
  0.0 37.0 %hyena.1 = bf16[256,256]{1,0:T(8,128)(2,1)S(1)} custom-call(bf16[256,256]{1,0:T(8,128)(2,1)} %gate_hbm.1, bf16[256,256]{1,0:T(8,128)(2,1)} %key_hbm.1, bf16[256,256]{1,0:T(8,128)(2,1)} %value_hbm.1, f32[9,256]{1,0:T(8,128)} %taps_hbm.1, f32[1,256]{1,0:T(1,128)} %bitcast.5, f32[16,256]{1,0:T(8,128)} %bitcast.3, f32[16,256]{1,0:T(8,128)} %bitcast.4, ...), custom_call_target="tpu_custom_call" | custom-call | tf_op jit(solution)/shard_map/hyena/pallas_call | solution.py:620
  37.0 0.7 %copy.10 = bf16[256,256]{1,0:T(8,128)(2,1)} copy(bf16[256,256]{1,0:T(8,128)(2,1)S(1)} %hyena.1) | data formatting | bytes 262144

commit v7 on v6

--- a/solution.py
+++ b/solution.py
@@ -71,6 +71,7 @@
     lead_rep,
     gathered,
     acc,
+    total,
     other_acc,
     in_sem,
     z_s,
@@ -592,11 +593,11 @@
             arrive(second, dist, (0, 1, 2))
             first_half(dist)
         last = list(range(1, half + 1))
-    acc[1] += product(last, 1)
-    send(acc.at[1], other_acc, sum_s.at[0], sum_r.at[0], (seq, sibling))
+    total[...] = (acc[1] + product(last, 1)).astype(BF16)
+    send(total, other_acc, sum_s.at[0], sum_r.at[0], (seq, sibling))
     acc[0] += product(last, 0)
     landed(other_acc, sum_r.at[0])
-    acc[0] += other_acc[...]
+    acc[0] += other_acc[...].astype(F32)
     out_ref[...] = jnp.dot(acc[0].astype(BF16), perm[...], preferred_element_type=F32).astype(BF16)
 
     for d in range(1, NZ):
@@ -608,7 +609,7 @@
     all_left(second, (0, 1, 2))
     for b in range(ny):
         left(columns(b, 1 - core), sib_s.at[b])
-    left(acc.at[1], sum_s.at[0])
+    left(total, sum_s.at[0])
 
 
 def body(nseq, nchan, gate, key, value, taps, gain, rates, residues, weight):
@@ -655,7 +656,8 @@
             pltpu.VMEM((ny, MODES, CHUNKS, LANES), F32),
             pltpu.VMEM((ny, toks, chans), BF16),
             pltpu.VMEM((2, weight.shape[0], toks), F32),
-            pltpu.VMEM((weight.shape[0], toks), F32),
+            pltpu.VMEM((weight.shape[0], toks), BF16),
+            pltpu.VMEM((weight.shape[0], toks), BF16),
             dma((7,)),
             dma((max(NZ - 1, 1),)),
             dma((max(NZ - 1, 1),)),

time: 37.9 us -> 37.7 us (level)
  the two profiles are of different devices: /device:TPU:5 before, /device:TPU:69 now
where the time goes in v7:
time: 37.7 us; the launch traced here: 37.5 us
  Pallas kernels  36.8 us (98%)
  local copies, waits for them, and re-layouts  0.66 us (2%)
    pallas_call x1, Pallas kernels, body(): pl.pallas_call(functools.partial(kernel, nseq, nchan), out_shape=pltpu.VM...  36.8 us

profile of v7, /device:TPU:69, one launch (start us, length us, event | category | flops | bytes accessed | tf_op | source)
XLA Modules:
  0.0 37.5 jit_solution(17612674859442206799)
XLA Ops:
  0.0 36.8 %hyena.1 = bf16[256,256]{1,0:T(8,128)(2,1)S(1)} custom-call(bf16[256,256]{1,0:T(8,128)(2,1)} %gate_hbm.1, bf16[256,256]{1,0:T(8,128)(2,1)} %key_hbm.1, bf16[256,256]{1,0:T(8,128)(2,1)} %value_hbm.1, f32[9,256]{1,0:T(8,128)} %taps_hbm.1, f32[1,256]{1,0:T(1,128)} %bitcast.5, f32[16,256]{1,0:T(8,128)} %bitcast.3, f32[16,256]{1,0:T(8,128)} %bitcast.4, ...), custom_call_target="tpu_custom_call" | custom-call | tf_op jit(solution)/shard_map/hyena/pallas_call | solution.py:621
  36.8 0.7 %copy.10 = bf16[256,256]{1,0:T(8,128)(2,1)} copy(bf16[256,256]{1,0:T(8,128)(2,1)S(1)} %hyena.1) | data formatting | bytes 262144

commit v8 on v6

--- a/solution.py
+++ b/solution.py
@@ -106,11 +106,11 @@
     loads = []
     for n, (src, dst) in enumerate(
         (
+            (key_hbm, key_v),
+            (value_hbm, value_v),
             (rates_hbm, rates_v),
             (res_hbm, res_v),
             (taps_hbm, taps_v),
-            (key_hbm, key_v),
-            (value_hbm, value_v),
             (gate_hbm, gate_v),
             (gain_hbm, gain_v),
         )
@@ -181,8 +181,8 @@
     col = lax.broadcasted_iota(jnp.int32, (toks, toks), 1)
     perm[...] = jnp.where(col == (row % CHUNKS) * blocks + row // CHUNKS, 1.0, 0.0).astype(BF16)
     k8 = lax.broadcasted_iota(jnp.int32, (CHUNKS, chans), 0).astype(F32) * float(blocks) + 1.0
-    loads[0].wait()
-    loads[1].wait()
+    loads[2].wait()
+    loads[3].wait()
     r_c = rates_v[...]
     w_c = res_v[...] * jnp.sqrt(r_c)
     w_v[...] = w_c
@@ -200,7 +200,7 @@
 
     at_k0 = lax.broadcasted_iota(jnp.int32, (CHUNKS, chans), 0) == 0
     tail = CHUNKS * (blocks - 2)
-    loads[2].wait()
+    loads[4].wait()
 
     def taps_of(m):
         return [taps_v[3 * m + j : 3 * m + j + 1, :] for j in range(3)]
@@ -220,13 +220,13 @@
         return result, tap[1] * last + tap[2] * prev, tap[2] * last
 
     own = zbuf.at[z]
-    loads[3].wait()
+    loads[0].wait()
     key_short, q0, q1 = short(1, key_v)
     own[16:17, :] = key_short[0:1]
     own[17:18, :] = key_short[CHUNKS : CHUNKS + 1]
     own[20:21, :] = q0
     own[21:22, :] = q1
-    loads[4].wait()
+    loads[1].wait()
     value_short, q0, q1 = short(2, value_v)
     own[18:19, :] = value_short[0:1]
     own[19:20, :] = value_short[CHUNKS : CHUNKS + 1]

time: 37.9 us -> 37.8 us (level)
  no operation moved by 1% of the time
where the time goes in v8:
time: 37.8 us; the launch traced here: 37.7 us
  Pallas kernels  37 us (98%)
  local copies, waits for them, and re-layouts  0.66 us (2%)
    pallas_call x1, Pallas kernels, body(): pl.pallas_call(functools.partial(kernel, nseq, nchan), out_shape=pltpu.VM...  37 us

profile of v8, /device:TPU:5, one launch (start us, length us, event | category | flops | bytes accessed | tf_op | source)
XLA Modules:
  0.0 37.7 jit_solution(2073331578821835331)
XLA Ops:
  0.0 37.0 %hyena.1 = bf16[256,256]{1,0:T(8,128)(2,1)S(1)} custom-call(bf16[256,256]{1,0:T(8,128)(2,1)} %gate_hbm.1, bf16[256,256]{1,0:T(8,128)(2,1)} %key_hbm.1, bf16[256,256]{1,0:T(8,128)(2,1)} %value_hbm.1, f32[9,256]{1,0:T(8,128)} %taps_hbm.1, f32[1,256]{1,0:T(1,128)} %bitcast.5, f32[16,256]{1,0:T(8,128)} %bitcast.3, f32[16,256]{1,0:T(8,128)} %bitcast.4, ...), custom_call_target="tpu_custom_call" | custom-call | tf_op jit(solution)/shard_map/hyena/pallas_call | solution.py:620
  37.0 0.7 %copy.10 = bf16[256,256]{1,0:T(8,128)(2,1)} copy(bf16[256,256]{1,0:T(8,128)(2,1)S(1)} %hyena.1) | data formatting | bytes 262144
